TPU v7x, 32 devices: a whole 2x2x4 slice. The times are simulated.
32 devices in a mesh: seq: 16 (over z, x, core), dp: 2 (over y).
Axes of the slice: x: 2, y: 2, z: 4, core: 2. Of those that a mesh axis runs over, the one named last changes fastest.
Arguments:
- tokens: bfloat16 [2, 6272, 1024], P('dp', 'seq'), may hold values from -6 to 6
- clip_start: int32 [2, 32], P('dp', 'seq'), may hold values from 0 to 28, as said below
- frames: int32 [2, 32], P('dp', 'seq'), may hold values from 8 to 32, as said below
- positions: int32 [2, 3, 6272], P('dp', None, 'seq'), may hold values from 0 to 15, as said below
- first_gain: float32 [1024], replicated, may hold values from 0.5 to 1.5
- first_offset: float32 [1024], replicated, may hold values from -3 to 3
- triple_weight: bfloat16 [1024, 3072], replicated, may hold values from -0.1875 to 0.1875
- triple_bias: float32 [3072], replicated, may hold values from -0.75 to 0.75
- output_weight: bfloat16 [1024, 1024], replicated, may hold values from -3 to 3
- output_bias: float32 [1024], replicated, may hold values from -1.5 to 1.5
- second_gain: float32 [1024], replicated, may hold values from 0.5 to 1.5
- second_offset: float32 [1024], replicated, may hold values from -3 to 3
- expand_weight: bfloat16 [1024, 4096], replicated, may hold values from -0.1875 to 0.1875
- expand_bias: float32 [4096], replicated, may hold values from -3 to 3
- reduce_weight: bfloat16 [4096, 1024], replicated, may hold values from -0.09375 to 0.09375
- reduce_bias: float32 [1024], replicated, may hold values from -1.5 to 1.5
- cotangent: bfloat16 [2, 6272, 1024], P('dp', 'seq'), may hold values from -6 to 6
Outputs:
- result: bfloat16 [2, 6272, 1024], P('dp', 'seq')
- input_grad: float32 [2, 6272, 1024], P('dp', 'seq')
- grad_first_gain: float32 [1024], P(('seq', 'dp'))
- grad_first_offset: float32 [1024], P(('seq', 'dp'))
- grad_triple_weight: float32 [1024, 3072], P(('seq', 'dp'))
- grad_query_key_bias: float32 [2048], P(('seq', 'dp'))
- grad_value_bias: float32 [1024], P(('seq', 'dp'))
- grad_output_weight: float32 [1024, 1024], P(('seq', 'dp'))
- grad_output_bias: float32 [1024], P(('seq', 'dp'))
- grad_second_gain: float32 [1024], P(('seq', 'dp'))
- grad_second_offset: float32 [1024], P(('seq', 'dp'))
- grad_expand_weight: float32 [1024, 4096], P(('seq', 'dp'))
- grad_expand_bias: float32 [4096], P(('seq', 'dp'))
- grad_reduce_weight: float32 [4096, 1024], P(('seq', 'dp'))
- grad_reduce_bias: float32 [1024], P(('seq', 'dp'))
Inputs may be any that keep to these rules, and one draw needn't show every extreme that they name: `clip_start`: each group's 32 slabs are split into whole clips of 4, 8 or 16 slabs that begin at multiples of 4; every slab of a clip holds the clip's first slab, and every group has a clip of 16 slabs. `frames`: twice the number of slabs of the slab's clip. `positions`: row 0 is the token's slab minus its clip's first slab; rows 1 and 2 are the token's row and column in its 14 x 14 frame plus an offset of 0 to 2 that is one for each clip and direction.
All inputs are finite; a program needn't handle non-finite values.
Results may differ from a plain program's by a relative error of at most 0.023.
Values may be sent and summed in bfloat16 or wider, within the bound.
No kernel may reach another device: no remote copies, remote signals or barrier semaphores. Data moves between devices by JAX's collectives and lax.ppermute only.
A program may use at most 384 MiB of HBM per device.

v0:
```python
import jax
import jax.numpy as jnp
from jax import lax
from jax.experimental import pallas as pl
from jax.experimental.pallas import tpu as pltpu
from jax.sharding import PartitionSpec as P

HEAD_DIM = 64
CLIP_MIN = 4
CLIP_MAX = 16
EPSILON = 1e-06
MASKED = 1e30
SECTIONS = ((0, 10), (20, 11), (42, 11))
LANES = 128
F32 = jnp.float32
BF16 = jnp.bfloat16
VMEM_LIMIT = 63 * 2**20
Q_TILE = 256
SAFE_ABOVE = 60.0
BACK_SHARE = (3, 4)


def dot(left, right):
    return jnp.dot(left, right, preferred_element_type=F32)


def dot_cols(left, right):
    return lax.dot_general(left, right, (((1,), (1,)), ((), ())), preferred_element_type=F32)


def dot_rows(left, right):
    return lax.dot_general(left, right, (((0,), (0,)), ((), ())), preferred_element_type=F32)


def cost(micros):
    return pl.CostEstimate(flops=int(micros * 1.15e9), bytes_accessed=2**20, transcendentals=0)


def params(sz=None, mib=0):
    if sz is not None and sz.n <= 16:
        return pltpu.CompilerParams(vmem_limit_bytes=mib * 2**20)
    return pltpu.CompilerParams(vmem_limit_bytes=VMEM_LIMIT)


def lane_index(shape):
    return lax.broadcasted_iota(jnp.int32, shape, len(shape) - 1)


def swap_halves(pair):
    return pltpu.roll(pair, HEAD_DIM, 1)


def rotate_pair(pair, cos_lanes, sin_lanes, inverse):
    lane = lane_index((1, LANES)) % HEAD_DIM
    sign = -1.0 if inverse else 1.0
    total = pair * cos_lanes
    for half in (10, 11):
        first = jnp.zeros(lane.shape, jnp.bool_)
        second = jnp.zeros(lane.shape, jnp.bool_)
        for begin_at, count in SECTIONS:
            if count == half:
                first = first | ((lane >= begin_at) & (lane < begin_at + half))
                second = second | ((lane >= begin_at + half) & (lane < begin_at + 2 * half))
        minus = jnp.where(first, -sign, 0.0)
        plus = jnp.where(second, sign, 0.0)
        total = total + pltpu.roll(pair, LANES - half, 1) * (sin_lanes * minus)
        total = total + pltpu.roll(pair, half, 1) * (sin_lanes * plus)
    return total


def lane_tables(positions):
    angles = jnp.zeros((positions.shape[1], LANES), F32)
    for section, (begin_at, count) in enumerate(SECTIONS):
        frequency = jnp.power(10000.0, -jnp.arange(count, dtype=F32) / count)
        in_head = jnp.zeros((HEAD_DIM,), F32)
        in_head = in_head.at[begin_at : begin_at + count].set(frequency)
        in_head = in_head.at[begin_at + count : begin_at + 2 * count].set(frequency)
        lanes = jnp.tile(in_head, LANES // HEAD_DIM)
        angles = angles + positions[section].astype(F32)[:, None] * lanes[None, :]
    return jnp.cos(angles), jnp.sin(angles)


def all_places(sz, corners):
    slabs = corners.shape[1] // 3
    per_slab = sz.rows // slabs
    side = int(round(per_slab**0.5))
    inside = jnp.arange(per_slab)
    steps = jnp.stack([jnp.zeros_like(inside), inside // side, inside % side])
    places = corners.reshape(sz.n, slabs, 3).transpose(0, 2, 1)[..., None] + steps[None, :, None, :]
    return places.reshape(sz.n, 3, sz.rows)


def all_turns(places):
    spots = jnp.arange(16)
    table = []
    for section in range(len(SECTIONS)):
        only = jnp.where(jnp.arange(len(SECTIONS))[:, None] == section, spots[None, :], 0)
        cos, sin = lane_tables(only)
        lane = jnp.arange(LANES)
        begin_at, count = SECTIONS[section]
        inside = (lane % HEAD_DIM >= begin_at) & (lane % HEAD_DIM < begin_at + 2 * count)
        table.append(jnp.where(inside, jnp.where(lane < HEAD_DIM, cos, sin), 0.0))
    table = jnp.concatenate(table, axis=0)
    hit = places.transpose(0, 2, 1)[..., None] == spots
    hit = hit.reshape(hit.shape[:2] + table.shape[:1]).astype(F32)
    hit = jnp.pad(hit, ((0, 0), (0, -hit.shape[1] % 16), (0, 0))).reshape(-1, table.shape[0])
    return jnp.dot(hit, table, precision=lax.Precision.HIGHEST)


def slab_bounds(clip_start, frames, first_slab, group_slabs):
    slab_index = first_slab + jnp.arange(clip_start.shape[-1], dtype=jnp.int32)
    unit_base = slab_index // CLIP_MIN * CLIP_MIN
    lower_slab = jnp.maximum(
        jnp.maximum(jnp.minimum(clip_start, slab_index), unit_base - (CLIP_MAX - CLIP_MIN)), 0
    )
    upper_slab = jnp.minimum(
        jnp.minimum(jnp.maximum(clip_start + frames // 2, slab_index + 1), unit_base + CLIP_MAX),
        group_slabs,
    )
    return lower_slab, upper_slab


def norm_parts(rows):
    centred = rows - jnp.mean(rows, axis=-1, keepdims=True)
    spread = jnp.mean(centred * centred, axis=-1, keepdims=True)
    scale = lax.rsqrt(spread + EPSILON)
    return centred * scale, scale


def norm_back(grad, rows, gain):
    unit, scale = norm_parts(rows)
    inner = grad * gain
    part = scale * (
        inner
        - jnp.mean(inner, axis=-1, keepdims=True)
        - unit * jnp.mean(inner * unit, axis=-1, keepdims=True)
    )
    return part, jnp.sum(grad * unit, axis=0, keepdims=True), jnp.sum(grad, axis=0, keepdims=True)


class Sizes:
    def __init__(self, rows, width, ff, n, m, slabs):
        self.rows = rows
        self.width = width
        self.ff = ff
        self.n = n
        self.m = m
        self.heads = width // HEAD_DIM
        self.rep = n // self.heads
        self.shards = n * m
        self.bits = (n // 2).bit_length() - 1
        self.per_unit = CLIP_MIN // slabs
        self.units = n // self.per_unit
        self.slot = (rows + 15) // 16 * 16
        self.unit_rows = self.slot * self.per_unit
        self.tokens = self.slot * n
        self.fold = (rows // 2 + 15) // 16 * 16
        self.rest = rows - self.fold
        self.msg = self.slot + self.fold


def pad_rows(block, count):
    if block.shape[0] == count:
        return block
    return jnp.concatenate([block, jnp.zeros((count - block.shape[0], block.shape[1]), F32)], axis=0)


def fold_head(block, sz, right):
    low = block[: sz.fold]
    high = pad_rows(block[sz.fold :], sz.fold)
    left = lane_index(low.shape) < HEAD_DIM
    if right:
        folded = jnp.where(left, swap_halves(low), high)
    else:
        folded = jnp.where(left, low, swap_halves(high))
    return folded


def project_kernel(sz, tok, gain, offset, wq, wk, wv, bq, bk, bv, cos, sin, meta, msg, normed_out):
    step = pl.program_id(0)

    @pl.when(step == 0)
    def _():
        unit, _ = norm_parts(tok[...].astype(F32))
        rows = (unit * gain[...] + offset[...]).astype(BF16)
        normed_out[0 : sz.rows, :] = rows
        normed_out[sz.rows :, :] = jnp.zeros((sz.slot - sz.rows, sz.width), BF16)

    normed = normed_out[0 : sz.rows, :]
    query = dot(normed, wq[...]) + bq[...]
    key = dot(normed, wk[...]) + bk[...]
    value = dot(normed, wv[...]) + bv[...]
    left = lane_index((sz.rows, LANES)) < HEAD_DIM
    spare = sz.slot - sz.rows
    facts = jnp.concatenate([jnp.zeros((sz.fold - 8, LANES), F32), meta[...]], axis=0)
    for pair in range(query.shape[1] // LANES):
        cols = slice(pair * LANES, (pair + 1) * LANES)
        q_pair = rotate_pair(query[:, cols], cos[...], sin[...], False) * 0.125
        k_pair = rotate_pair(key[:, cols], cos[...], sin[...], False)
        v_pair = value[:, cols]
        both = (jnp.where(left, k_pair, swap_halves(v_pair)), jnp.where(left, swap_halves(k_pair), v_pair))
        for head in range(2):
            tail = jnp.where(left[:spare], both[head][sz.rows - spare :], 0.0)
            folded = fold_head(q_pair, sz, head == 1) + facts
            rows = jnp.concatenate([both[head], tail, folded], axis=0)
            msg[2 * pair + head] = rows.astype(BF16)


def project(sz, tokens, gain, offset, weight, bias, cos, sin, meta):
    cols = 256
    steps = sz.width // cols
    whole = lambda shape: pl.BlockSpec(shape, lambda j: (0,) * len(shape))
    part = lambda k: pl.BlockSpec((sz.width, cols), lambda j: (0, k * steps + j))
    part_bias = lambda k: pl.BlockSpec((1, cols), lambda j: (0, k * steps + j))
    heads = cols // HEAD_DIM
    return pl.pallas_call(
        lambda *refs: project_kernel(sz, *refs),
        grid=(steps,),
        in_specs=[whole((sz.rows, sz.width)), whole((1, sz.width)), whole((1, sz.width))]
        + [part(0), part(1), part(2), part_bias(0), part_bias(1), part_bias(2)]
        + [whole((sz.rows, LANES)), whole((sz.rows, LANES)), whole((8, LANES))],
        out_specs=[
            pl.BlockSpec((heads, sz.msg, LANES), lambda j: (j, 0, 0)),
            whole((sz.slot, sz.width)),
        ],
        out_shape=[
            jax.ShapeDtypeStruct((sz.heads, sz.msg, LANES), BF16),
            jax.ShapeDtypeStruct((sz.slot, sz.width), BF16),
        ],
        compiler_params=params(),
        cost_estimate=cost(8),
        name="project",
    )(tokens, gain, offset, weight, weight, weight, bias, bias, bias, cos, sin, meta)


def unfold_slot(folded, sz, right):
    wide = folded.astype(F32)
    left = lane_index(wide.shape) < HEAD_DIM
    keep = ~left if right else left
    swapped = swap_halves(wide)
    low, high = (swapped, wide) if right else (wide, swapped)
    return (
        jnp.where(keep, low, 0.0).astype(BF16),
        jnp.where(keep, high, 0.0)[: sz.slot - sz.fold].astype(BF16),
    )


def unfold_into(target, at, folded, sz, right):
    low, high = unfold_slot(folded, sz, right)
    target[pl.ds(at, sz.fold), :] = low
    target[pl.ds(at + sz.fold, sz.slot - sz.fold), :] = high


def loop(count, body):
    def step(index, carry):
        body(index)
        return carry

    lax.fori_loop(0, count, step, 0)


def attend_kernel(sz, first, count, recv, out, kept, qs, kvs, ones_v):
    def unpack(src):
        at = pl.multiple_of(src * sz.slot, 16)
        unfold_into(qs, at, recv[src, sz.slot :, :], sz, False)
        kv = recv[src, 0 : sz.slot, :]
        kvs[pl.ds(at, sz.slot), :] = kv
        left = lane_index((1, LANES)) < HEAD_DIM
        real = lax.broadcasted_iota(jnp.int32, (sz.slot, 1), 0) < sz.rows
        one = jnp.where(real, 1.0, 0.0)
        ones_v[pl.ds(at, sz.slot), :] = jnp.where(left, one, kv.astype(F32)).astype(BF16)

    loop(sz.n, unpack)
    qs[sz.tokens :, :] = jnp.zeros((Q_TILE, LANES), BF16)
    kept[sz.tokens :, :] = jnp.zeros((Q_TILE, LANES), F32)

    def one(unit):
        rows = pl.ds(pl.multiple_of(unit * sz.unit_rows, 16), sz.unit_rows)
        begin = pl.multiple_of(first[unit] * sz.unit_rows, 16)

        def keep(shift, mixed):
            total = mixed[:, 0:1]
            left = lane_index((1, LANES)) < HEAD_DIM
            kept[rows, :] = jnp.where(left, shift + jnp.log(total), mixed * (1.0 / total))

        for span in (1, 2, 4):

            @pl.when(count[unit] == span)
            def _():
                clip = pl.ds(begin, span * sz.unit_rows)
                some = dot_cols(qs[rows, :], kvs[pl.ds(begin, 2 * LANES), :])
                shift = jnp.max(some, axis=1, keepdims=True)
                scores = dot_cols(qs[rows, :], kvs[clip, :])
                prob = jnp.exp(scores - shift).astype(BF16)
                keep(shift, dot(prob, ones_v[clip, :]))
                above = jnp.max(jnp.max(scores, axis=1, keepdims=True) - shift)

                @pl.when(above > SAFE_ABOVE)
                def _():
                    scores = dot_cols(qs[rows, :], kvs[clip, :])
                    peak = jnp.max(scores, axis=1, keepdims=True)
                    prob = jnp.exp(scores - peak).astype(BF16)
                    keep(peak, dot(prob, ones_v[clip, :]))

    loop(sz.units, one)

    def pack(src):
        at = pl.multiple_of(src * sz.slot, 16)
        out[src] = fold_head(kept[pl.ds(at, sz.slot), :][: sz.rows], sz, True).astype(BF16)
        left = lane_index((sz.slot - sz.rows, LANES)) < HEAD_DIM
        kept[pl.ds(at + sz.rows, sz.slot - sz.rows), :] = jnp.where(left, MASKED, 0.0)

    loop(sz.n, pack)


def attend(sz, first, count, recv):
    smem = pl.BlockSpec(memory_space=pltpu.SMEM)
    vmem = pl.BlockSpec(memory_space=pltpu.VMEM)
    shape = jax.ShapeDtypeStruct
    return pl.pallas_call(
        lambda *refs: attend_kernel(sz, *refs),
        in_specs=[smem, smem, vmem],
        out_specs=[vmem] * 4,
        out_shape=[
            shape((sz.n, sz.fold, LANES), BF16),
            shape((sz.tokens + Q_TILE, LANES), F32),
            shape((sz.tokens + Q_TILE, LANES), BF16),
            shape((sz.tokens, LANES), BF16),
        ],
        scratch_shapes=[pltpu.VMEM((sz.tokens, LANES), BF16)],
        compiler_params=params(),
        cost_estimate=cost(32),
        name="attend",
    )(first, count, recv)


def back_tiles(sz, part, first, count, qs, kvs, dos, kept, grad_q, grad_kv, key_t):
    def one(unit):
        begin = pl.multiple_of(unit * sz.unit_rows, 16)
        for span in (1, 2, 4):

            @pl.when((count[unit] == span) & (first[unit] == unit))
            def _():
                length = span * sz.unit_rows
                clip = pl.ds(begin, length)
                turned = kvs[clip, :].astype(F32).T[:HEAD_DIM]
                real = lax.rem(lane_index((1, length)), sz.slot) < sz.rows
                key_t[:, 0:length] = jnp.where(real, turned, 0.0).astype(BF16)

                def q_tile(t, carry):
                    rows = pl.ds(pl.multiple_of(begin + t * Q_TILE, 16), Q_TILE)
                    query = qs[rows, :]
                    grad = dos[rows, :]
                    kept_rows = kept[rows, :]
                    left = lane_index((Q_TILE, LANES)) < HEAD_DIM
                    turned = jnp.where(left, kept_rows, kept_rows * grad.astype(F32)).T
                    inside = lane_index((1, Q_TILE)) < length - t * Q_TILE
                    log_total = jnp.where(inside, turned[0:1, :], MASKED)
                    delta = jnp.sum(turned[HEAD_DIM:, :], axis=0, keepdims=True)
                    keys = kvs[clip, :]
                    prob = jnp.exp(dot_cols(keys, query) - log_total)
                    grad_prob = dot_cols(keys, grad)
                    grad_scores = (prob * (grad_prob - delta)).astype(BF16)
                    grad_kv[clip, :] += dot(grad_scores, query) + dot(prob.astype(BF16), grad)
                    grad_query = dot(key_t[:, 0:length], grad_scores) * 0.125
                    grad_query = jnp.concatenate([grad_query, jnp.zeros_like(grad_query)], axis=0).T
                    if part == 1:
                        own = lax.broadcasted_iota(jnp.int32, (Q_TILE, 1), 0) < length - t * Q_TILE
                        grad_query = jnp.where(own, grad_query, grad_q[rows, :])
                    grad_q[rows, :] = grad_query
                    return carry

                tiles = (length + Q_TILE - 1) // Q_TILE
                middle = (tiles * BACK_SHARE[0] + BACK_SHARE[1] - 1) // BACK_SHARE[1]
                lax.fori_loop(*((0, middle) if part == 0 else (middle, tiles)), q_tile, 0)

    loop(sz.units, one)


def back_first_kernel(sz, first, count, recv_grad, qs, kvs, kept, dos, grad_q, grad_kv, key_t):
    dos[sz.tokens :, :] = jnp.zeros((Q_TILE, LANES), BF16)

    def unpack(src):
        at = pl.multiple_of(src * sz.slot, 16)
        unfold_into(dos, at, recv_grad[src], sz, True)
        grad_kv[pl.ds(at, sz.slot), :] = jnp.zeros((sz.slot, LANES), F32)

    loop(sz.n, unpack)
    back_tiles(sz, 0, first, count, qs, kvs, dos, kept, grad_q, grad_kv, key_t)


def back_last_kernel(
    sz, first, count, dos, qs, kvs, kept, grad_q_in, grad_kv_in, turns, out, grad_q, grad_kv, key_t
):
    def copy(src):
        rows = pl.ds(pl.multiple_of(src * sz.slot, 16), sz.slot)
        grad_q[rows, :] = grad_q_in[rows, :]
        grad_kv[rows, :] = grad_kv_in[rows, :]

    loop(sz.n, copy)
    back_tiles(sz, 1, first, count, qs, kvs, dos, kept, grad_q, grad_kv, key_t)

    def pack(src):
        rows = pl.ds(pl.multiple_of(src * sz.slot, 16), sz.slot)
        kv = grad_kv[rows, :]
        left = lane_index((1, LANES)) < HEAD_DIM
        real = lax.broadcasted_iota(jnp.int32, (sz.slot, 1), 0) < sz.rows
        both = jnp.where(left, grad_q[rows, :], swap_halves(kv))
        table = turns[rows, :]
        other = swap_halves(table)
        both = rotate_pair(both, jnp.where(left, table, other), jnp.where(left, other, table), True)
        out[src, 0 : sz.slot, :] = jnp.where(real, jnp.where(left, swap_halves(both), kv), 0.0).astype(BF16)
        out[src, sz.slot :, :] = fold_head(both[: sz.rows], sz, False).astype(BF16)

    loop(sz.n, pack)


def attend_back_first(sz, first, count, recv_grad, qs, kvs, kept):
    smem = pl.BlockSpec(memory_space=pltpu.SMEM)
    vmem = pl.BlockSpec(memory_space=pltpu.VMEM)
    shape = jax.ShapeDtypeStruct
    return pl.pallas_call(
        lambda *refs: back_first_kernel(sz, *refs),
        in_specs=[smem, smem] + [vmem] * 4,
        out_specs=[vmem] * 3,
        out_shape=[
            shape((sz.tokens + Q_TILE, LANES), BF16),
            shape((sz.tokens + Q_TILE, LANES), F32),
            shape((sz.tokens, LANES), F32),
        ],
        scratch_shapes=[pltpu.VMEM((HEAD_DIM, CLIP_MAX // CLIP_MIN * sz.unit_rows), BF16)],
        compiler_params=params(sz, 18),
        cost_estimate=cost(40),
        name="attend_back_first",
    )(first, count, recv_grad, qs, kvs, kept)


def attend_back_last(sz, first, count, dos, qs, kvs, kept, grad_q, grad_kv, turns):
    smem = pl.BlockSpec(memory_space=pltpu.SMEM)
    vmem = pl.BlockSpec(memory_space=pltpu.VMEM)
    shape = jax.ShapeDtypeStruct
    return pl.pallas_call(
        lambda *refs: back_last_kernel(sz, *refs),
        in_specs=[smem, smem] + [vmem] * 7,
        out_specs=vmem,
        out_shape=shape((sz.n, sz.msg, LANES), BF16),
        scratch_shapes=[
            pltpu.VMEM((sz.tokens + Q_TILE, LANES), F32),
            pltpu.VMEM((sz.tokens, LANES), F32),
            pltpu.VMEM((HEAD_DIM, CLIP_MAX // CLIP_MIN * sz.unit_rows), BF16),
        ],
        compiler_params=params(sz, 18),
        cost_estimate=cost(20),
        name="attend_back_last",
    )(first, count, dos, qs, kvs, kept, grad_q, grad_kv, turns)


def triple_grad_kernel(sz, grads, normed, out, total):
    step = pl.program_id(0)
    high = sz.slot - sz.fold
    part_kv = jnp.zeros((LANES, sz.width), F32)
    part_q = jnp.zeros((HEAD_DIM, sz.width), F32)
    sums = jnp.zeros((1, 2 * LANES), F32)
    for src in range(grads.shape[0]):
        key_value = grads[src, 0 : sz.slot, :]
        query = grads[src, sz.slot :, :]
        part_kv = part_kv + dot_rows(key_value, normed[src])
        part_q = part_q + dot_rows(query, normed[src, 0 : sz.fold, :])[:HEAD_DIM]
        part_q = part_q + dot_rows(query[:high], normed[src, sz.fold :, :])[HEAD_DIM:]
        sum_kv = jnp.sum(key_value.astype(F32), axis=0, keepdims=True)
        sum_q = jnp.sum(query.astype(F32), axis=0, keepdims=True)
        sums = sums + jnp.concatenate([sum_kv, sum_q + swap_halves(sum_q)], axis=1)

    @pl.when(step == 0)
    def _():
        total[...] = jnp.zeros_like(total)

    total[0:LANES, :] += part_kv
    total[LANES : LANES + HEAD_DIM, :] += part_q
    total[2 * LANES :, 0 : 2 * LANES] += jnp.broadcast_to(sums, (8, 2 * LANES))

    @pl.when(step == pl.num_programs(0) - 1)
    def _():
        few = sz.width // sz.shards
        bias = total[2 * LANES : 2 * LANES + 1, 0 : 2 * LANES]
        place = lax.broadcasted_iota(jnp.int32, (sz.width, 1), 0) % few
        left = lane_index((1, LANES)) < HEAD_DIM
        out[:, 0:LANES] = total[0:LANES, :].T
        queries = total[LANES : 2 * LANES, :].T
        kv_row, q_row = bias[:, 0:LANES], bias[:, LANES:]
        side = jnp.where(place == 0, swap_halves(kv_row), jnp.where(place == 1, kv_row, 0.0))
        side = jnp.where(place == 2, q_row, side)
        out[:, LANES:] = jnp.where(left, queries, side)


def triple_grad(sz, grads, normed_all):
    shape = jax.ShapeDtypeStruct
    last = sz.n // 2 - 1
    return pl.pallas_call(
        lambda *refs: triple_grad_kernel(sz, *refs),
        grid=(sz.n // 2,),
        in_specs=[
            pl.BlockSpec((2, sz.msg, LANES), lambda j: (j, 0, 0)),
            pl.BlockSpec((2, sz.slot, sz.width), lambda j: (jnp.where(j % 2 == 0, j // 2, last - j // 2), 0, 0)),
        ],
        out_specs=pl.BlockSpec((sz.width, 2 * LANES), lambda j: (0, 0)),
        out_shape=shape((sz.width, 2 * LANES), F32),
        scratch_shapes=[pltpu.VMEM((2 * LANES + 8, sz.width), F32)],
        compiler_params=params(sz, 54),
        cost_estimate=cost(1),
        name="triple_grad",
    )(grads, normed_all)


def choose(pieces, index):
    picked = pieces[0]
    for at in range(1, len(pieces)):
        picked = jnp.where(index == at, pieces[at], picked)
    return picked


def core_cols(block, width, side):
    count = block.shape[1] // (2 * width)
    groups = [block[:, g * width : (g + 1) * width] for g in range(2 * count)]
    return jnp.concatenate([choose(groups[2 * g : 2 * g + 2], side) for g in range(count)], axis=1)


def feed_kernel(sz, place, tok, heads_in, wo, bo, gain, offset, we, be, wr, br, cot, *refs):
    result, grad_hidden, msg, shared, grad_exp, act_sent, act_own = refs[:7]
    grad_be, grad_gain, grad_offset, grad_bo, grad_br = refs[7:12]
    hidden, reduced, grad_normed = refs[12:]
    step = pl.program_id(0)
    core = place[0]
    left = lane_index((sz.fold, LANES)) < HEAD_DIM
    normed = shared.at[:, 0 : sz.width]
    attended = shared.at[:, sz.width : 2 * sz.width]

    @pl.when(step == 0)
    def _():
        for pair in range(sz.heads // 2):
            a = heads_in[2 * pair, 0 : sz.fold, :].astype(F32)
            b = heads_in[2 * pair + 1, 0 : sz.fold, :].astype(F32)
            low = jnp.where(left, a, swap_halves(b))
            high = jnp.where(left, swap_halves(a), b)[: sz.rest]
            both = jnp.concatenate([low, high], axis=0)
            attended[:, pair * LANES : (pair + 1) * LANES] = both.astype(BF16)
        rows = tok[...].astype(F32) + (dot(attended[...], wo[...]) + bo[...])
        hidden[...] = rows
        unit, _ = norm_parts(rows)
        normed[...] = (unit * gain[...] + offset[...]).astype(BF16)
        reduced[...] = jnp.zeros_like(reduced)
        grad_normed[...] = jnp.zeros_like(grad_normed)

    expanded = dot(normed[...], we[...]) + be[...]
    below = 0.5 * (1.0 + lax.erf(expanded * 0.7071067811865476))
    bell = jnp.exp(expanded * expanded * -0.5) * 0.3989422804014327
    activated = expanded * below
    slope = below + expanded * bell
    act_low = activated.astype(BF16)
    reduced[...] += dot(act_low, wr[...])
    grad_expanded = (dot_cols(cot[...], wr[...]) * slope).astype(BF16)
    grad_be[...] = jnp.sum(grad_expanded.astype(F32), axis=0, keepdims=True)
    grad_normed[...] += dot_cols(grad_expanded, we[...])
    act_own[...] = core_cols(activated, sz.ff // sz.n, core).astype(BF16)
    act_sent[...] = core_cols(activated, sz.ff // sz.n, 1 - core).astype(BF16)
    grad_exp[...] = grad_expanded

    @pl.when(step == pl.num_programs(0) - 1)
    def _():
        rows = hidden[...]
        out_grad = cot[...].astype(F32)
        result[...] = (rows + (reduced[...] + br[...])).astype(BF16)
        part, gain_part, offset_part = norm_back(grad_normed[...], rows, gain[...])
        total = out_grad + part
        grad_hidden[...] = total
        grad_gain[...] = gain_part
        grad_offset[...] = offset_part
        grad_br[...] = jnp.sum(out_grad, axis=0, keepdims=True)
        low = total.astype(BF16)
        shared[:, 2 * sz.width : 3 * sz.width] = low
        grad_bo[...] = jnp.sum(low.astype(F32), axis=0, keepdims=True)
        for quarter in range(4):
            wide = sz.width // 4
            grad_attended = dot_cols(low, wo[quarter * wide : (quarter + 1) * wide, :])
            for pair in range(wide // LANES):
                both = grad_attended[:, pair * LANES : (pair + 1) * LANES]
                head = 2 * (quarter * (wide // LANES) + pair)
                msg[head] = fold_head(both, sz, False).astype(BF16)
                msg[head + 1] = fold_head(both, sz, True).astype(BF16)


def feed(sz, place, tokens, heads_in, wo, bo, gain, offset, we, be, wr, br, cot):
    span = 512
    steps = sz.ff // span
    whole = lambda *shape: pl.BlockSpec(shape, lambda j: (0,) * len(shape), pipeline_mode=pl.Buffered(1))
    shape = jax.ShapeDtypeStruct
    vector = whole(1, sz.width)
    vector_out = shape((1, sz.width), F32)
    return pl.pallas_call(
        lambda *refs: feed_kernel(sz, *refs),
        grid=(steps,),
        in_specs=[
            pl.BlockSpec(memory_space=pltpu.SMEM),
            whole(sz.rows, sz.width),
            whole(sz.heads, sz.fold, LANES),
            whole(sz.width, sz.width),
            vector,
            vector,
            vector,
            pl.BlockSpec((sz.width, span), lambda j: (0, j)),
            pl.BlockSpec((1, span), lambda j: (0, j)),
            pl.BlockSpec((span, sz.width), lambda j: (j, 0)),
            vector,
            whole(sz.rows, sz.width),
        ],
        out_specs=[
            whole(sz.rows, sz.width),
            whole(sz.rows, sz.width),
            whole(sz.heads, sz.fold, LANES),
            whole(sz.rows, 3 * sz.width),
            pl.BlockSpec((sz.rows, span), lambda j: (0, j)),
            pl.BlockSpec((sz.rows, span // 2), lambda j: (0, j)),
            pl.BlockSpec((sz.rows, span // 2), lambda j: (0, j)),
            pl.BlockSpec((1, span), lambda j: (0, j)),
            vector,
            vector,
            vector,
            vector,
        ],
        out_shape=[
            shape((sz.rows, sz.width), BF16),
            shape((sz.rows, sz.width), F32),
            shape((sz.heads, sz.fold, LANES), BF16),
            shape((sz.rows, 3 * sz.width), BF16),
            shape((sz.rows, sz.ff), BF16),
            shape((sz.rows, sz.ff // 2), BF16),
            shape((sz.rows, sz.ff // 2), BF16),
            shape((1, sz.ff), F32),
            vector_out,
            vector_out,
            vector_out,
            vector_out,
        ],
        scratch_shapes=[pltpu.VMEM((sz.rows, sz.width), F32)] * 3,
        compiler_params=params(),
        cost_estimate=cost(28),
        name="feed",
    )(place, tokens, heads_in, wo, bo, gain, offset, we, be, wr, br, cot)


def weights_kernel(sz, place, act, act_got, cot, cot_got, back, back_got, norm, norm_got, *refs):
    att, att_got, low, low_got = refs[:4]
    wr_own, wr_sent, first_own, first_sent, next_own, next_sent = refs[4:10]
    wo_out = refs[10 : 10 + sz.m]
    norm_t, norm_t_got = refs[10 + sz.m :]
    step = pl.program_id(0)
    core, low_bit, mine_dp = place[0], place[1], place[1 + sz.bits]
    per = sz.width // sz.n

    def core_rows(block):
        turned = block[...].astype(F32).T.reshape(sz.n // 2, 2, per, sz.rows)
        return choose([turned[:, 0], turned[:, 1]], core).reshape(sz.width // 2, sz.rows).astype(BF16)

    @pl.when(step == 0)
    def _():
        norm_t[...] = core_rows(norm)
        norm_t_got[...] = core_rows(norm_got)
        grad_wo = dot(core_rows(att), low[...]) + dot(core_rows(att_got), low_got[...])
        grad_wo = grad_wo.reshape(sz.n // 2, sz.m, per // sz.m, sz.width)
        sides = [grad_wo[:, q] for q in range(sz.m)]
        for by in range(sz.m):
            wo_out[by][...] = choose(sides, lax.rem(mine_dp + by, sz.m)).astype(BF16)

    groups = act.shape[1] // (sz.ff // sz.n)
    grad_wr = (dot_rows(act[...], cot[...]) + dot_rows(act_got[...], cot_got[...])).astype(BF16)
    grad_wr = grad_wr.reshape(groups, sz.ff // sz.n, sz.width)
    if groups == 1:

        @pl.when(step % 2 == low_bit)
        def _():
            wr_own[...] = grad_wr

        @pl.when(step % 2 != low_bit)
        def _():
            wr_sent[...] = grad_wr

    else:
        wr_own[...] = choose([grad_wr[0:1], grad_wr[1:2]], low_bit)
        wr_sent[...] = choose([grad_wr[0:1], grad_wr[1:2]], 1 - low_bit)
    grad_we = dot(norm_t[...], back[...]) + dot(norm_t_got[...], back_got[...])

    def split(bit, own, sent):
        above, below = sz.n // 4 >> bit, (1 << bit) * sz.m
        parts = grad_we.reshape(above, 2, below, per // sz.m, grad_we.shape[1])
        sides = [parts[:, 0], parts[:, 1]]
        own[...] = choose(sides, place[1 + bit]).astype(BF16).reshape(own.shape)
        sent[...] = choose(sides, 1 - place[1 + bit]).astype(BF16).reshape(sent.shape)

    @pl.when(step < pl.num_programs(0) // 2)
    def _():
        split(2, first_own, first_sent)

    @pl.when(step >= pl.num_programs(0) // 2)
    def _():
        split(1, next_own, next_sent)


def weights(sz, place, act, act_got, cot, cot_got, back, back_got, shared, shared_got):
    span = sz.width
    steps = sz.ff // span
    fan = sz.ff // sz.width
    half = sz.n // 2
    few = sz.width // sz.shards
    whole = lambda *shape: pl.BlockSpec(shape, lambda j: (0,) * len(shape))
    column = lambda k: pl.BlockSpec((sz.rows, sz.width), lambda j: (0, k))
    block = pl.BlockSpec((sz.rows, span), lambda j: (0, j))
    act_block = pl.BlockSpec((sz.rows, span // 2), lambda j: (0, j))
    shape = jax.ShapeDtypeStruct
    groups = half // steps
    wr_block = pl.BlockSpec((1, sz.ff // sz.n, sz.width), lambda j: (j * groups // 2, 0, 0))
    wr_out = shape((half // 2, sz.ff // sz.n, sz.width), BF16)
    wo_dims = (half, few, sz.width)
    last_j = steps // 2 - 1
    first_block = pl.BlockSpec((half // 2 * sz.m, 1, few, span), lambda j: (0, jnp.minimum(j, last_j), 0, 0))
    next_block = pl.BlockSpec((half // 2 * sz.m, 1, few, span), lambda j: (0, jnp.maximum(j - last_j - 1, 0), 0, 0))
    we_out = shape((half // 2 * sz.m, fan // 2, few, sz.width), BF16)
    return pl.pallas_call(
        lambda *refs: weights_kernel(sz, *refs),
        grid=(steps,),
        in_specs=[
            pl.BlockSpec(memory_space=pltpu.SMEM),
            act_block,
            act_block,
            whole(sz.rows, sz.width),
            whole(sz.rows, sz.width),
            block,
            block,
        ]
        + [column(k // 2) for k in range(6)],
        out_specs=[wr_block] * 2 + [first_block] * 2 + [next_block] * 2 + [whole(*wo_dims)] * sz.m,
        out_shape=[wr_out] * 2 + [we_out] * 4 + [shape(wo_dims, BF16)] * sz.m,
        scratch_shapes=[pltpu.VMEM((sz.width // 2, sz.rows), BF16)] * 2,
        compiler_params=params(),
        cost_estimate=cost(10),
        name="weights",
    )(place, act, act_got, cot, cot_got, back, back_got, *([shared, shared_got] * 3))


def finish_kernel(sz, back, wq, wk, wv, tok, gain, grad_hidden, input_grad, grad_normed):
    step = pl.program_id(0)
    left = lane_index((sz.rows, LANES)) < HEAD_DIM
    left_fold = lane_index((sz.fold, LANES)) < HEAD_DIM
    queries, keys, values = [], [], []
    for pair in range(wq.shape[1] // LANES):
        kv_a = back[2 * pair, 0 : sz.rows, :].astype(F32)
        kv_b = back[2 * pair + 1, 0 : sz.rows, :].astype(F32)
        q_a = back[2 * pair, sz.slot : sz.slot + sz.fold, :].astype(F32)
        q_b = back[2 * pair + 1, sz.slot : sz.slot + sz.fold, :].astype(F32)
        low = jnp.where(left_fold, q_a, swap_halves(q_b))
        high = jnp.where(left_fold, swap_halves(q_a), q_b)[: sz.rest]
        queries.append(jnp.concatenate([low, high], axis=0).astype(BF16))
        keys.append(jnp.where(left, kv_a, swap_halves(kv_b)).astype(BF16))
        values.append(jnp.where(left, swap_halves(kv_a), kv_b).astype(BF16))
    total = jnp.zeros((sz.rows, sz.width), F32)
    for parts, weight in ((queries, wq), (keys, wk), (values, wv)):
        total = total + dot_cols(jnp.concatenate(parts, axis=1), weight[...])

    @pl.when(step == 0)
    def _():
        grad_normed[...] = total

    @pl.when(step > 0)
    def _():
        grad_normed[...] += total

    @pl.when(step == pl.num_programs(0) - 1)
    def _():
        part, _, _ = norm_back(grad_normed[...], tok[...].astype(F32), gain[...])
        input_grad[...] = grad_hidden[...] + part


def finish(sz, back, weight, tokens, gain, grad_hidden):
    cols = 512
    steps = sz.width // cols
    whole = lambda *shape: pl.BlockSpec(shape, lambda j: (0,) * len(shape))
    part = lambda k: pl.BlockSpec((sz.width, cols), lambda j: (0, k * steps + j))
    return pl.pallas_call(
        lambda *refs: finish_kernel(sz, *refs),
        grid=(steps,),
        in_specs=[
            pl.BlockSpec((cols // HEAD_DIM, sz.msg, LANES), lambda j: (j, 0, 0)),
            part(0),
            part(1),
            part(2),
            whole(sz.rows, sz.width),
            whole(1, sz.width),
            whole(sz.rows, sz.width),
        ],
        out_specs=whole(sz.rows, sz.width),
        out_shape=jax.ShapeDtypeStruct((sz.rows, sz.width), F32),
        scratch_shapes=[pltpu.VMEM((sz.rows, sz.width), F32)],
        compiler_params=params(sz, 54),
        cost_estimate=cost(10),
        name="finish",
    )(back, weight, weight, weight, tokens, gain, grad_hidden)


def pick(array, axis, index):
    return lax.dynamic_index_in_dim(array, index, axis, keepdims=False)


def after(value, *others):
    return lax.optimization_barrier((value,) + others)[0]


class Side:
    def __init__(self, sz, labels, rows, arrays):
        self.dims = [(label, sz.m if label == "dp" else 2) for label in labels]
        self.rows = rows
        self.width = sz.width
        self.arrays = list(arrays)

    def split(self, label):
        at = [name for name, _ in self.dims].index(label)
        before, after_it = 1, self.rows
        for _, size in self.dims[:at]:
            before *= size
        for _, size in self.dims[at + 1 :]:
            after_it *= size
        count = self.dims[at][1]
        self.dims = self.dims[:at] + self.dims[at + 1 :]
        return before, count, after_it

    def total(self):
        return sum(array.astype(F32) for array in self.arrays).reshape(self.rows, self.width)


def halve_kernel(shapes, place, *refs):
    at = 0
    outs = sum(adds * count for adds, count in shapes)
    for adds, count in shapes:
        for _ in range(count):
            total = refs[at][:, 0].astype(F32)
            for more in range(1, adds):
                total = total + refs[at + more][:, 0].astype(F32)
            refs[outs][...] = total.astype(BF16)
            at += adds
            outs += 1


def halve(sz, place, sides, labels):
    parts = [side.split(label) for side, label in zip(sides, labels)]
    grid = 2 if all(before % 2 == 0 for before, _, _ in parts) else 1
    ins, in_specs, out_specs, out_shape = [], [], [], []
    for side, label, (before, count, rest) in zip(sides, labels, parts):
        which = 1 + sz.bits if label == "dp" else 1 + label
        for by in range(count):
            for array in side.arrays:
                ins.append(array.reshape(before, count, rest, sz.width))
                in_specs.append(
                    pl.BlockSpec(
                        (before // grid, 1, rest, sz.width),
                        lambda g, place, which=which, by=by, count=count: (g, lax.rem(place[which] + by, count), 0, 0),
                    )
                )
            out_specs.append(pl.BlockSpec((before // grid, rest, sz.width), lambda g, place: (g, 0, 0)))
            out_shape.append(jax.ShapeDtypeStruct((before, rest, sz.width), BF16))
    shapes = [(len(side.arrays), count) for side, (_, count, _) in zip(sides, parts)]
    outs = pl.pallas_call(
        lambda *refs: halve_kernel(shapes, *refs),
        grid_spec=pltpu.PrefetchScalarGridSpec(
            num_scalar_prefetch=1, grid=(grid,), in_specs=in_specs, out_specs=out_specs
        ),
        out_shape=out_shape,
        compiler_params=params(sz, 20),
        cost_estimate=cost(4),
        name="halve",
    )(place, *ins)
    sent = []
    for side, (_, count, _) in zip(sides, parts):
        side.arrays = [outs[0]]
        sent.append(list(outs[1:count]))
        outs = outs[count:]
    return sent


def send(sz, label, blocks):
    if label == "dp":
        return [
            lax.ppermute(block, "dp", [(i, (i + by + 1) % sz.m) for i in range(sz.m)])
            for by, block in enumerate(blocks)
        ]
    bit = 2 << label
    return [lax.ppermute(block, "seq", [(i, i ^ bit) for i in range(sz.n)]) for block in blocks]


def swap(sz, block, by):
    return block if by == 0 else lax.ppermute(block, "seq", [(i, i ^ by) for i in range(sz.n)])


def trade_near(sz, blocks):
    me = lax.axis_index("seq")
    blocks = blocks.reshape((sz.n // 4, 4) + blocks.shape[1:])
    return jnp.stack([swap(sz, pick(blocks, 1, me % 4 ^ by), by) for by in range(4)], axis=1)


def trade_far(sz, near):
    me = lax.axis_index("seq")
    return jnp.stack([swap(sz, pick(near, 0, me // 4 ^ by), 4 * by) for by in range(sz.n // 4)], axis=0)


def last_kernel(sz, adds, spans, place, far, gain, offset, weight, *refs):
    ins, outs = refs[: sum(adds)], refs[sum(adds) :]
    totals = []
    for count in adds:
        total = ins[0][...].astype(F32)
        for more in range(1, count):
            total = total + ins[more][...].astype(F32)
        totals.append(total)
        ins = ins[count:]
    wr, we, wo, wt, bias_all, gain_one, offset_one = outs[:7]
    few = sz.width // sz.shards
    wr[...] = totals[0]
    half = sz.ff // sz.width // 2
    for part in range(2 * half):
        rows = totals[1 + part // half][part % half * few : (part % half + 1) * few]
        we[:, part * sz.width : (part + 1) * sz.width] = rows
    wo[...] = totals[3]
    low = place[0] + 2 * place[1]
    high = place[2]
    for bit in range(2, sz.bits):
        high = high + place[1 + bit] * 2 ** (bit - 1)

    def piece(src):
        return far[jnp.bitwise_xor(high, src // 4), jnp.bitwise_xor(low, src % 4)].astype(F32)

    left = lane_index((1, LANES)) < HEAD_DIM
    small = jnp.zeros((8, LANES), F32)
    along = jnp.zeros((8, LANES), F32)
    moved = jnp.zeros((few, 1), F32)
    for pair in range(sz.heads // 2):
        a = piece(2 * pair * sz.rep)
        b = piece((2 * pair + 1) * sz.rep)
        kv_a, kv_b, q_a, q_b = a[:, :LANES], b[:, :LANES], a[:, LANES:], b[:, LANES:]
        along = along + q_a[:8] + q_b[:8]
        blocks = (
            jnp.where(left, q_a, swap_halves(q_b)),
            jnp.where(left, kv_a, swap_halves(kv_b)),
            jnp.where(left, swap_halves(kv_a), kv_b),
        )
        side = jnp.where(left, swap_halves(q_a[:8]), q_b[:8])
        for part, row in ((0, 2), (1, 0), (2, 1)):
            cols = slice(part * sz.width + pair * LANES, part * sz.width + (pair + 1) * LANES)
            wt[:, cols] = blocks[part]
            bias_all[:, cols] = side[row : row + 1]
            rows = weight[:, cols].astype(F32) * side[row : row + 1]
            moved = moved + jnp.sum(rows, axis=1, keepdims=True)
    for src in range(sz.n):
        small = small + piece(src)[:8, LANES:]
    along = swap_halves(along)[7:8]
    small = swap_halves(small)
    small = jnp.concatenate([small[3 + row : 4 + row, :HEAD_DIM] for row in range(4)], axis=1)
    moved = jnp.broadcast_to(moved, (few, LANES)).T[0:1]
    offset_one[...] = moved
    gain_one[...] = (along[:, :few] - offset[0] * moved) / gain[0]
    at = 0
    for out, span in zip(outs[7:], spans):
        out[...] = small[:, at : at + span]
        at += span


def last(sz, place, sides, far, gain, offset, weight, spans):
    few = sz.width // sz.shards
    shard = lambda g, place: (place[2 + sz.bits], 0, 0)
    whole = lambda *shape: pl.BlockSpec(shape, lambda g, place: (0,) * len(shape))
    ins, in_specs = [], []
    for side in sides:
        for array in side.arrays:
            ins.append(array.reshape(side.rows, sz.width))
            in_specs.append(whole(side.rows, sz.width))
    out_dims = [(sides[0].rows, sz.width), (few, sz.ff), (few, sz.width), (few, 3 * sz.width), (1, 3 * sz.width)]
    out_dims = out_dims + [(1, few), (1, few)] + [(1, span) for span in spans]
    return pl.pallas_call(
        lambda *refs: last_kernel(sz, [len(side.arrays) for side in sides], spans, *refs),
        grid_spec=pltpu.PrefetchScalarGridSpec(
            num_scalar_prefetch=1,
            grid=(1,),
            in_specs=[
                whole(*far.shape),
                pl.BlockSpec((1, 1, few), shard),
                pl.BlockSpec((1, 1, few), shard),
                pl.BlockSpec((few, 3 * sz.width), lambda g, place: (place[2 + sz.bits], 0)),
            ]
            + in_specs,
            out_specs=[whole(*dims) for dims in out_dims],
        ),
        out_shape=[jax.ShapeDtypeStruct(dims, F32) for dims in out_dims],
        compiler_params=params(sz, 50),
        cost_estimate=cost(5),
        name="last",
    )(place, far, gain.reshape(sz.shards, 1, few), offset.reshape(sz.shards, 1, few), weight, *ins)


def per_device(
    tokens,
    clip_start,
    frames,
    positions,
    first_gain,
    first_offset,
    triple_weight,
    triple_bias,
    output_weight,
    output_bias,
    second_gain,
    second_offset,
    expand_weight,
    expand_bias,
    reduce_weight,
    reduce_bias,
    cotangent,
):
    rows, width = tokens.shape[1:]
    ff = expand_weight.shape[1]
    n = lax.axis_size("seq")
    m = lax.axis_size("dp")
    slabs = clip_start.shape[1]
    sz = Sizes(rows, width, ff, n, m, slabs)
    shards = n * m
    group_slabs = n * slabs
    lower, upper = slab_bounds(clip_start[0], frames[0], lax.axis_index("seq") * slabs, group_slabs)
    first_unit = lower[0] // CLIP_MIN
    unit_count = (upper[0] - lower[0]) // CLIP_MIN
    corners = positions[0].reshape(3, slabs, -1)[:, :, 0].T.reshape(-1)
    meta = jnp.concatenate([jnp.stack([first_unit, unit_count]), corners])[:8, None]
    meta = jnp.where(jnp.arange(LANES) < HEAD_DIM, 0, meta).astype(F32)
    cos, sin = lane_tables(positions[0])
    row = lambda vector: vector.reshape(1, -1)
    me, mine_dp = lax.axis_index("seq"), lax.axis_index("dp")
    place = jnp.stack([me % 2] + [me // (2 << bit) % 2 for bit in range(sz.bits)] + [mine_dp, me * m + mine_dp])
    swap_core = lambda block: lax.ppermute(block, "seq", [(i, i ^ 1) for i in range(n)])

    def exchange(message):
        if sz.rep > 1:
            message = jnp.repeat(message, sz.rep, axis=0)
        return lax.all_to_all(message, "seq", 0, 0, tiled=True)

    cot_got = swap_core(cotangent[0])
    head = me // sz.rep * HEAD_DIM
    head_weight = [
        lax.dynamic_slice(triple_weight, (0, k * width + head), (width, HEAD_DIM)) for k in (1, 2, 0)
    ]
    head_weight = jnp.concatenate(head_weight + [jnp.zeros((width, HEAD_DIM), BF16)], axis=1)
    message, normed = project(
        sz, tokens[0], row(first_gain), row(first_offset), triple_weight, row(triple_bias), cos, sin, meta
    )
    recv = exchange(message)
    chips = list(range(0, n // 2, 2)) + list(range(n // 2 - 1, 0, -2))
    ring = [2 * chip + core for chip in chips for core in range(2)]
    normed_all = lax.all_gather(after(normed, recv), "seq", axis=0, tiled=False, axis_index_groups=[ring])
    facts = recv[:, sz.msg - 8 :, LANES - 1].astype(jnp.int32)
    unit_first, unit_span = facts[:: sz.per_unit, 0], facts[:: sz.per_unit, 1]
    turns = all_turns(all_places(sz, facts[:, 2:]))
    out_message, kept, qs, kvs = attend(sz, unit_first, unit_span, recv)
    heads_in = lax.all_to_all(out_message, "seq", 0, 0, tiled=True)[:: sz.rep]
    (
        result,
        grad_hidden,
        grad_message,
        shared,
        grad_exp,
        act_sent,
        act_own,
        grad_be,
        grad_second_gain,
        grad_second_offset,
        grad_bo,
        grad_br,
    ) = feed(
        sz,
        place,
        tokens[0],
        after(heads_in, turns),
        output_weight,
        row(output_bias),
        row(second_gain),
        row(second_offset),
        expand_weight,
        row(expand_bias),
        reduce_weight,
        row(reduce_bias),
        cotangent[0],
    )
    recv_grad = exchange(grad_message)
    half = n // 2
    fan = ff // width
    few = width // shards
    many = ff // shards
    wr_own, wr_sent, first_own, first_sent, next_own, next_sent, *wo_parts = weights(
        sz,
        place,
        act_own,
        swap_core(act_sent),
        cotangent[0],
        cot_got,
        grad_exp,
        swap_core(grad_exp),
        shared,
        swap_core(shared),
    )
    bits = list(range(sz.bits - 1, -1, -1))
    side_r = Side(sz, bits[:-1] + ["dp"], many, [wr_own])
    without = lambda label: [bit for bit in bits if bit != label] + ["dp"]
    side_e = Side(sz, without(2), many // 2, [first_own])
    side_f = Side(sz, without(1), many // 2, [next_own])
    side_o = Side(sz, bits, few, [wo_parts[0]])
    sides = [side_r, side_e, side_f, side_o]
    sent = [[wr_sent], [first_sent], [next_sent], wo_parts[1:]]
    rounds = [(0, 2, 1, "dp"), (1, "dp", 0, 2), ("dp", 0, "dp", 0), (2, 1, 2, 1)]
    rounds = rounds + [(bit,) * 4 for bit in range(3, sz.bits)]

    def move(labels):
        return [send(sz, label, blocks) for label, blocks in zip(labels, sent)]

    def add(got, marker):
        for side, blocks in zip(sides, got):
            side.arrays = side.arrays + list(after(blocks, marker))

    got = move(rounds[0])
    dos, grad_q, grad_kv = attend_back_first(
        sz, unit_first, unit_span, after(recv_grad, wo_parts[0]), qs, kvs, kept
    )
    add(got, grad_kv)
    sent = halve(sz, place, sides, rounds[1])
    got = move(rounds[1])
    back_message = attend_back_last(
        sz, unit_first, unit_span, after(dos, sent), qs, kvs, kept, grad_q, grad_kv, turns
    )
    back = lax.all_to_all(after(back_message, got), "seq", 0, 0, tiled=True)[:: sz.rep]
    add(got, back_message)
    sent = halve(sz, place, sides, rounds[2])
    got = move(rounds[2])
    head_grad = triple_grad(sz, after(back_message, sent), normed_all)
    columns = [grad_bo, grad_second_gain, grad_second_offset, grad_be, grad_br]
    columns = [column.reshape(shards, -1) for column in after(columns, back_message)]
    spans = [column.shape[1] for column in columns]
    head_grad = after(head_grad, got)
    small = jnp.concatenate(columns, axis=1)
    small = jnp.pad(small, ((0, 0), (0, 4 * HEAD_DIM - small.shape[1]))).reshape(shards, 4, HEAD_DIM)
    along = jnp.sum(head_grad * head_weight.astype(F32), axis=1).reshape(shards, 1, few)
    along = jnp.pad(along, ((0, 0), (0, 0), (0, HEAD_DIM - few)))
    spare = jnp.concatenate([small, along], axis=1)
    spare = jnp.pad(spare, ((0, 0), (3, few - 8), (3 * HEAD_DIM, 0)))
    head_parts = (head_grad.reshape(shards, few, 4 * HEAD_DIM) + spare).reshape(n, m, few, 4 * HEAD_DIM)
    head_sum = pick(head_parts, 1, mine_dp)
    for by in range(1, m):
        block = pick(head_parts, 1, (mine_dp + by) % m).astype(BF16)
        head_sum = head_sum + lax.ppermute(block, "dp", [(i, (i + by) % m) for i in range(m)]).astype(F32)
    near = trade_near(sz, head_sum.astype(BF16))
    back = after(back, near)
    add(got, back_message)
    for step, labels in enumerate(rounds[3:]):
        if step > 0:
            add(got, back)
        sent = after(halve(sz, place, sides, labels), back)
        got = move(labels)
    far = trade_far(sz, near)
    input_grad = finish(
        sz, after(back, sent, far), triple_weight, tokens[0], row(first_gain), grad_hidden
    )
    add(got, input_grad)
    (
        out_wr,
        out_we,
        out_wo,
        out_wt,
        bias_all,
        gain_one,
        offset_one,
        *vectors,
    ) = last(sz, place, sides, far, first_gain, first_offset, triple_weight, spans)
    shard = me * m + mine_dp
    bias_qk = lax.dynamic_slice(bias_all[0], (shard * 2 * few,), (2 * few,))
    bias_v = lax.dynamic_slice(bias_all[0], (2 * width + shard * few,), (few,))
    gain_one, offset_one = gain_one[0], offset_one[0]
    bias_o, gain_two, offset_two, bias_e, bias_r = [vector[0] for vector in vectors]
    return (
        result[None],
        input_grad[None],
        gain_one,
        offset_one,
        out_wt,
        bias_qk,
        bias_v,
        out_wo,
        bias_o,
        gain_two,
        offset_two,
        out_we,
        bias_e,
        out_wr,
        bias_r,
    )


def solution(mesh):
    sharded = P("dp", "seq", None)
    placed = (
        (sharded, P("dp", "seq"), P("dp", "seq"), P("dp", None, "seq"))
        + (P(),) * 12
        + (sharded,)
    )
    vector = P(("seq", "dp"))
    matrix = P(("seq", "dp"), None)
    return jax.shard_map(
        per_device,
        mesh=mesh,
        in_specs=placed,
        out_specs=(sharded, sharded, vector, vector, matrix, vector, vector, matrix, vector)
        + (vector, vector, matrix, vector, matrix, vector),
        check_vma=False,
    )
```

profile of v0, /device:TPU:0, one launch (start us, length us, event | category | flops | bytes accessed | tf_op | source)
XLA Modules:
  0.0 399.0 jit_solution(4192138270671621588)
XLA Ops:
  11.2 1.6 fusion.2
  12.8 9.4 %project.1 = (bf16[16,608,128]{2,1,0:T(8,128)(2,1)}, bf16[400,1024]{1,0:T(8,128)(2,1)}) custom-call(bf16[392,1024]{1,0:T(8,128)(2,1)} %bitcast.249, f32[1,1024]{1,0:T(1,128)} %bitcast.237, f32[1,1024]{1,0:T(1,128)} %bitcast.236, bf16[1024,3072]{1,0:T(8,128)(2,1)} %refs_4_.3, bf16[1024,3072]{1,0:T(8,128)(2,1)} %refs_4_.3, bf16[1024,3072]{1,0:T(8,128)(2,1)} %refs_4_.3, ...), custom_call_target="tpu_custom_call" | custom-call | flops 9200000000 | bytes 1048576 | tf_op jit(solution)/shard_map/project/pallas_call | solution.py:216
  22.2 63.6 %all_to_all.20.refs_2_ = bf16[16,608,128]{2,1,0:T(8,128)(2,1)S(1)} all-to-all(bf16[16,608,128]{2,1,0:T(8,128)(2,1)} %get-tuple-element.330), channel_id=1, replica_groups=mesh['seq'=16,'dp'=2] {'seq'}, dimensions={0} | all-to-all | bytes 4980736 | tf_op jit(solution)/shard_map/all_to_all | solution.py:1046
  86.0 1.2 copy-done.34
  88.7 28.5 %attend.1 = (bf16[16,208,128]{2,1,0:T(8,128)(2,1)}, f32[6656,128]{1,0:T(8,128)}, bf16[6656,128]{1,0:T(8,128)(2,1)}, bf16[6400,128]{1,0:T(8,128)(2,1)}) custom-call(s32[8]{0:T(128)} %bitcast.216, s32[8]{0:T(128)} %bitcast.219, bf16[16,608,128]{2,1,0:T(8,128)(2,1)} %copy-done.34), custom_call_target="tpu_custom_call" | custom-call | flops 36800000000 | bytes 1048576 | tf_op jit(solution)/shard_map/attend/pallas_call | solution.py:320
  117.1 4.6 %all-to-all-start.1 = ((bf16[16,208,128]{2,1,0:T(8,128)(2,1)}), bf16[16,208,128]{2,1,0:T(8,128)(2,1)S(1)}, u32[]{:S(2)}, u32[]{:S(2)}) async-start(bf16[16,208,128]{2,1,0:T(8,128)(2,1)} %get-tuple-element.331), calls=%async_computation.1 | async-start | bytes 1703936 | tf_op jit(solution)/shard_map/all_to_all | solution.py:1065
  124.0 1.1 reshape.693
  125.2 4.4 %fusion.4.refs_8_ = f32[6400,128]{1,0:T(8,128)} fusion(pred[6400,48]{0,1:T(8,128)(4,1)S(1)} %reshape.693, f32[16,128]{1,0:T(8,128)S(1)} %get-tuple-element.447, f32[16,128]{1,0:T(8,128)S(1)} %get-tuple-element.446, f32[16,128]{1,0:T(8,128)S(1)} %get-tuple-element.445), kind=kOutput, calls=%fused_computation.22 | convolution fusion | flops 471871488 | bytes 3608576 | tf_op jit(solution)/shard_map/dot_general | solution.py:107
  129.6 25.7 %all-to-all-done.1.refs_2_ = bf16[16,208,128]{2,1,0:T(8,128)(2,1)S(1)} async-done(((bf16[16,208,128]{2,1,0:T(8,128)(2,1)}), bf16[16,208,128]{2,1,0:T(8,128)(2,1)S(1)}, u32[]{:S(2)}, u32[]{:S(2)}) %all-to-all-start.1) | async-done | bytes 852000 | tf_op jit(solution)/shard_map/all_to_all | solution.py:1065
  156.2 26.9 %feed.1 = (bf16[392,1024]{1,0:T(8,128)(2,1)}, f32[392,1024]{1,0:T(8,128)}, bf16[16,208,128]{2,1,0:T(8,128)(2,1)}, bf16[392,3072]{1,0:T(8,128)(2,1)}, bf16[392,40...) custom-call(s32[6]{0:T(128)} %stack.64.refs_0_, ...), custom_call_target="tpu_custom_call" | custom-call | flops 32199999488 | bytes 1048576 | tf_op jit(solution)/shard_map/feed/pallas_call | solution.py:599
  184.2 3.8 all-to-all-start.2
  188.0 8.2 %collective-permute-done.1.refs_4_ = bf16[392,1024]{1,0:T(8,128)(2,1)} collective-permute-done((bf16[392,1024]{1,0:T(8,128)(2,1)}, bf16[392,1024]{1,0:T(8,128)(2,1)}, u32[]{:S(2)}, u32[]{:S(2)}) %collective-permute-start.1) | collective-permute-done | bytes 802848 | tf_op jit(solution)/shard_map/ppermute | solution.py:1041
  196.3 1.4 copy-done.43
  197.7 18.3 %weights.1 = (bf16[4,256,1024]{2,1,0:T(8,128)(2,1)}, bf16[4,256,1024]{2,1,0:T(8,128)(2,1)}, bf16[8,2,32,1024]{3,2,1,0:T(8,128)(2,1)}, bf16[8,2,32,1024]{3,2,1,0:...) custom-call(s32[6]{0:T(128)} %stack.64.refs_0_, ...), custom_call_target="tpu_custom_call" | custom-call | flops 11500000256 | bytes 1048576 | tf_op jit(solution)/shard_map/weights/pallas_call | solution.py:727
  216.0 1.6 collective-permute-start.7
  217.6 1.1 collective-permute-start.4
  218.8 2.0 copy-done.29
  220.7 1.5 copy-done.31
  222.2 1.4 copy-done.32
  223.6 37.5 %attend_back_first.1 = (bf16[6656,128]{1,0:T(8,128)(2,1)S(1)}, f32[6656,128]{1,0:T(8,128)S(1)}, f32[6400,128]{1,0:T(8,128)S(1)}) custom-call(s32[8]{0:T(128)S(1)} %bitcast.217, s32[8]{0:T(128)S(1)} %bitcast.220, bf16[16,208,128]{2,1,0:T(8,128)(2,1)S(1)} %all-to-all-done.2.refs_2_, bf16[6656,128]{1,0:T(8,128)(2,1)S(1)} %copy-done.31, ...), custom_call_target="tpu_custom_call" | custom-call | flops 46000001024 | bytes 1048576 | tf_op jit(solution)/shard_map/attend_back_first/pallas_call | solution.py:422
  261.2 2.3 collective-permute-done.6
  263.4 2.7 collective-permute-done.5
  266.2 1.6 halve.3
  268.6 1.7 collective-permute-start.11
  271.1 1.7 collective-permute-start.8
  272.9 20.2 %attend_back_last.1.refs_0_ = bf16[16,608,128]{2,1,0:T(8,128)(2,1)} custom-call(s32[8]{0:T(128)S(1)} %bitcast.218, s32[8]{0:T(128)S(1)} %bitcast.221, bf16[6656,128]{1,0:T(8,128)(2,1)S(1)} %get-tuple-element.361.refs_2_, bf16[6656,128]{1,0:T(8,128)(2,1)S(1)} %copy-done.31, bf16[6400,128]{1,0:T(8,128)(2,1)S(1)} %copy-done.33, f32[6656,128]{1,0:T(8,128)S(1)} %copy-done.30, ...), custom_call_target="tpu_custom_call" | custom-call | flops 23000000512 | bytes 1048576 | tf_op jit(solution)/shard_map/attend_back_last/pallas_call | solution.py:442
  294.6 5.2 %collective-permute-done.8 = bf16[2,256,1024]{2,1,0:T(8,128)(2,1)S(1)} collective-permute-done((bf16[2,256,1024]{2,1,0:T(8,128)(2,1)S(1)}, bf16[2,256,1024]{2,1,0:T(8,128)(2,1)S(1)}, u32[]{:S(2)}, u32[]{:S(2)}) %collective-permute-start.8) | collective-permute-done | bytes 1048608 | tf_op jit(solution)/shard_map/ppermute | solution.py:894
  299.9 4.4 %all-to-all-start.3 = ((bf16[16,608,128]{2,1,0:T(8,128)(2,1)}), bf16[16,608,128]{2,1,0:T(8,128)(2,1)}, u32[]{:S(2)}, u32[]{:S(2)}) async-start(bf16[16,608,128]{2,1,0:T(8,128)(2,1)} %attend_back_last.1.refs_0_), calls=%async_computation.3 | async-start | bytes 4980736 | tf_op jit(solution)/shard_map/all_to_all | solution.py:1139
  309.4 1.7 halve.4
  314.6 1.5 collective-permute-start.12
  316.1 1.8 collective-permute-start.13
  318.7 1.4 constant_dynamic-slice_fusion.6
  323.9 12.1 %triple_grad.1 = f32[1024,256]{1,0:T(8,128)} custom-call(bf16[16,608,128]{2,1,0:T(8,128)(2,1)} %attend_back_last.1.refs_0_, bf16[16,400,1024]{2,1,0:T(8,128)(2,1)} %bitcast.222), custom_call_target="tpu_custom_call" | custom-call | flops 1150000000 | bytes 1048576 | tf_op jit(solution)/shard_map/triple_grad/pallas_call | solution.py:499
  336.3 1.7 multiply_reduce_fusion
  338.2 2.5 pad_add_fusion
  341.8 1.3 collective-permute-start.16
  343.1 6.6 %collective-permute-done.16 = bf16[16,32,256]{2,1,0:T(8,128)(2,1)S(1)} collective-permute-done((bf16[16,32,256]{2,1,0:T(8,128)(2,1)S(1)}, bf16[16,32,256]{2,1,0:T(8,128)(2,1)S(1)}, u32[]{:S(2)}, u32[]{:S(2)}) %collective-permute-start.16) | collective-permute-done | bytes 262176 | tf_op jit(solution)/shard_map/ppermute | solution.py:1158
  351.0 2.5 collective-permute-start.18
  353.7 2.4 collective-permute-done.18
  356.1 1.4 collective-permute-done.19
  358.2 3.5 collective-permute-start.20
  361.7 2.4 collective-permute-start.22
  365.5 1.1 collective-permute-start.26
  368.2 1.2 collective-permute-done.21
  371.5 8.8 %finish.1 = f32[392,1024]{1,0:T(8,128)} custom-call(bf16[16,608,128]{2,1,0:T(8,128)(2,1)} %all-to-all-done.3.refs_0_, bf16[1024,3072]{1,0:T(8,128)(2,1)} %refs_4_.3, bf16[1024,3072]{1,0:T(8,128)(2,1)} %refs_4_.3, bf16[1024,3072]{1,0:T(8,128)(2,1)} %refs_4_.3, bf16[392,1024]{1,0:T(8,128)(2,1)} %bitcast.251, f32[1,1024]{1,0:T(1,128)} %bitcast.238, ...), custom_call_target="tpu_custom_call" | custom-call | flops 11500000256 | bytes 1048576 | tf_op jit(solution)/shard_map/finish/pallas_call | solution.py:787
  380.3 1.6 collective-permute-done.25
  381.9 5.5 %collective-permute-done.23 = bf16[1,128,1024]{2,1,0:T(8,128)(2,1)S(1)} collective-permute-done((bf16[1,128,1024]{2,1,0:T(8,128)(2,1)S(1)}, bf16[1,128,1024]{2,1,0:T(8,128)(2,1)S(1)}, u32[]{:S(2)}, u32[]{:S(2)}) %collective-permute-start.23) | collective-permute-done | bytes 262176 | tf_op jit(solution)/shard_map/ppermute | solution.py:894
  387.4 3.4 last.1
  (201 shorter events, 35.5 us)
Async XLA Ops:
  7.2 316.7 %all-gather.3.cloned.1.call-start = ((), (), s32[]{:S(2)}) async-start(), calls=%async_computation.4 | async-start | bytes 13926400 | tf_op jit(solution)/shard_map/all_gather | solution.py:1060
  117.1 38.2 %all-to-all-start.1 = ((bf16[16,208,128]{2,1,0:T(8,128)(2,1)}), bf16[16,208,128]{2,1,0:T(8,128)(2,1)S(1)}, u32[]{:S(2)}, u32[]{:S(2)}) async-start(bf16[16,208,128]{2,1,0:T(8,128)(2,1)} %get-tuple-element.331), calls=%async_computation.1 | async-start | bytes 1703936 | tf_op jit(solution)/shard_map/all_to_all | solution.py:1065
  183.1 13.1 %collective-permute-start.2 = (bf16[392,4096]{1,0:T(8,128)(2,1)}, bf16[392,4096]{1,0:T(8,128)(2,1)}, u32[]{:S(2)}, u32[]{:S(2)}) collective-permute-start(bf16[392,4096]{1,0:T(8,128)(2,1)} %get-tuple-element.337.refs_5_), channel_id=1, source_target_pairs={{0,2},{2,0},{4,6},{6,4},{8,10},{10,8},{12,14},{14,12},{16,18},{18,... | collective-permute-start | bytes 9633800 | tf_op jit(solution)/shard_map/ppermute | solution.py:1041
  183.2 13.1 %collective-permute-start.3 = (bf16[392,3072]{1,0:T(8,128)(2,1)}, bf16[392,3072]{1,0:T(8,128)(2,1)S(1)}, u32[]{:S(2)}, u32[]{:S(2)}) collective-permute-start(bf16[392,3072]{1,0:T(8,128)(2,1)} %get-tuple-element.338.refs_7_.refs_9_.refs_11_), channel_id=1, source_target_pairs={{0,2},{2,0},{4,6},{6,4},{8,10},{10,8},{12,14},{14,12},{16,18},{18,... | collective-permute-start | bytes 7225352 | tf_op jit(solution)/shard_map/ppermute | solution.py:1041
  183.7 12.6 %collective-permute-start = (bf16[392,2048]{1,0:T(8,128)(2,1)}, bf16[392,2048]{1,0:T(8,128)(2,1)}, u32[]{:S(2)}, u32[]{:S(2)}) collective-permute-start(bf16[392,2048]{1,0:T(8,128)(2,1)} %get-tuple-element.336), channel_id=1, source_target_pairs={{0,2},{2,0},{4,6},{6,4},{8,10},{10,8},{12,14},{14,12},{16,18},{18,... | collective-permute-start | bytes 4816904 | tf_op jit(solution)/shard_map/ppermute | solution.py:1041
  183.8 12.5 %collective-permute-start.1 = (bf16[392,1024]{1,0:T(8,128)(2,1)}, bf16[392,1024]{1,0:T(8,128)(2,1)}, u32[]{:S(2)}, u32[]{:S(2)}) collective-permute-start(bf16[392,1024]{1,0:T(8,128)(2,1)} %bitcast.247), channel_id=1, source_target_pairs={{0,2},{2,0},{4,6},{6,4},{8,10},{10,8},{12,14},{14,12},{16,18},{18,... | collective-permute-start | bytes 2408456 | tf_op jit(solution)/shard_map/ppermute | solution.py:1041
  184.2 31.8 %all-to-all-start.2 = ((bf16[16,208,128]{2,1,0:T(8,128)(2,1)}), bf16[16,208,128]{2,1,0:T(8,128)(2,1)S(1)}, u32[]{:S(2)}, u32[]{:S(2)}) async-start(bf16[16,208,128]{2,1,0:T(8,128)(2,1)} %get-tuple-element.334), calls=%async_computation.2 | async-start | bytes 1703936 | tf_op jit(solution)/shard_map/all_to_all | solution.py:1046
  197.7 21.1 %copy-start.27 = (s32[8,1]{0,1:T(1,128)S(1)}, s32[8,1]{0,1:T(1,128)}, u32[]{:S(2)}) copy-start(s32[8,1]{0,1:T(1,128)} %slice.245) | copy-start | bytes 100
  197.7 21.1 %copy-start.28 = (s32[8,1]{0,1:T(1,128)S(1)}, s32[8,1]{0,1:T(1,128)}, u32[]{:S(2)}) copy-start(s32[8,1]{0,1:T(1,128)} %slice.246) | copy-start | bytes 100
  216.0 45.2 %collective-permute-start.7 = (bf16[8,32,1024]{2,1,0:T(8,128)(2,1)}, bf16[8,32,1024]{2,1,0:T(8,128)(2,1)S(1)}, u32[]{:S(2)}, u32[]{:S(2)}) collective-permute-start(bf16[8,32,1024]{2,1,0:T(8,128)(2,1)} %get-tuple-element.355), channel_id=1, source_target_pairs={{0,1},{1,0},{2,3},{3,2},{4,5},{5,4},{6,7},{7,6},{8,9},{9,8},{10,11... | collective-permute-start | bytes 1572872 | tf_op jit(solution)/shard_map/ppermute | solution.py:890
  217.6 45.8 %collective-permute-start.6 = (bf16[8,2,32,1024]{3,2,1,0:T(8,128)(2,1)}, bf16[8,2,32,1024]{3,2,1,0:T(8,128)(2,1)S(1)}, u32[]{:S(2)}, u32[]{:S(2)}) collective-permute-start(bf16[8,2,32,1024]{3,2,1,0:T(8,128)(2,1)} %get-tuple-element.353), channel_id=1, source_target_pairs={{0,8},{2,10},{4,12},{6,14},{8,0},{10,2},{12,4},{14,6},{16,24},{18,... | collective-permute-start | bytes 3145736 | tf_op jit(solution)/shard_map/ppermute | solution.py:894
  217.6 48.5 %collective-permute-start.5 = (bf16[8,2,32,1024]{3,2,1,0:T(8,128)(2,1)}, bf16[8,2,32,1024]{3,2,1,0:T(8,128)(2,1)S(1)}, u32[]{:S(2)}, u32[]{:S(2)}) collective-permute-start(bf16[8,2,32,1024]{3,2,1,0:T(8,128)(2,1)} %get-tuple-element.350), channel_id=1, source_target_pairs={{0,16},{2,18},{4,20},{6,22},{8,24},{10,26},{12,28},{14,30},{16,0},... | collective-permute-start | bytes 3145736 | tf_op jit(solution)/shard_map/ppermute | solution.py:894
  217.6 48.5 %collective-permute-start.4 = (bf16[4,256,1024]{2,1,0:T(8,128)(2,1)}, bf16[4,256,1024]{2,1,0:T(8,128)(2,1)S(1)}, u32[]{:S(2)}, u32[]{:S(2)}) collective-permute-start(bf16[4,256,1024]{2,1,0:T(8,128)(2,1)} %get-tuple-element.346), channel_id=1, source_target_pairs={{0,4},{2,6},{4,0},{6,2},{8,12},{10,14},{12,8},{14,10},{16,20},{18,... | collective-permute-start | bytes 6291464 | tf_op jit(solution)/shard_map/ppermute | solution.py:894
  223.6 42.6 %copy-start = (bf16[4,256,1024]{2,1,0:T(8,128)(2,1)S(1)}, bf16[4,256,1024]{2,1,0:T(8,128)(2,1)}, u32[]{:S(2)}) copy-start(bf16[4,256,1024]{2,1,0:T(8,128)(2,1)} %get-tuple-element.345) | copy-start | bytes 6291460
  223.6 42.6 %copy-start.1 = (bf16[8,2,32,1024]{3,2,1,0:T(8,128)(2,1)S(1)}, bf16[8,2,32,1024]{3,2,1,0:T(8,128)(2,1)}, u32[]{:S(2)}) copy-start(bf16[8,2,32,1024]{3,2,1,0:T(8,128)(2,1)} %get-tuple-element.349) | copy-start | bytes 3145732
  223.6 42.6 %copy-start.2 = (bf16[8,2,32,1024]{3,2,1,0:T(8,128)(2,1)S(1)}, bf16[8,2,32,1024]{3,2,1,0:T(8,128)(2,1)}, u32[]{:S(2)}) copy-start(bf16[8,2,32,1024]{3,2,1,0:T(8,128)(2,1)} %get-tuple-element.352) | copy-start | bytes 3145732
  223.6 42.6 %copy-start.4 = (bf16[8,32,1024]{2,1,0:T(8,128)(2,1)S(1)}, bf16[8,32,1024]{2,1,0:T(8,128)(2,1)}, u32[]{:S(2)}) copy-start(bf16[8,32,1024]{2,1,0:T(8,128)(2,1)} %get-tuple-element.339) | copy-start | bytes 1572868
  223.6 42.6 %copy-start.5 = (s32[6]{0:T(128)S(1)}, s32[6]{0:T(128)}, u32[]{:S(2)}) copy-start(s32[6]{0:T(128)} %stack.64.refs_0_) | copy-start | bytes 76
  268.6 24.4 %copy-start.12 = (bf16[1,128,1024]{2,1,0:T(8,128)(2,1)}, bf16[1,128,1024]{2,1,0:T(8,128)(2,1)S(1)}, u32[]{:S(2)}) copy-start(bf16[1,128,1024]{2,1,0:T(8,128)(2,1)S(1)} %get-tuple-element.370) | copy-start | bytes 786436
  268.6 24.4 %collective-permute-start.11 = (bf16[1,128,1024]{2,1,0:T(8,128)(2,1)S(1)}, bf16[1,128,1024]{2,1,0:T(8,128)(2,1)S(1)}, u32[]{:S(2)}, u32[]{:S(2)}) collective-permute-start(bf16[1,128,1024]{2,1,0:T(8,128)(2,1)S(1)} %get-tuple-element.360), channel_id=1, source_target_pairs={{0,16},{2,18},{4,20},{6,22},{8,24},{10,26},{12,28},{14,30},{16,0},... | collective-permute-start | bytes 786440 | tf_op jit(solution)/shard_map/ppermute | solution.py:894
  270.3 23.5 %collective-permute-start.10 = (bf16[2,128,1024]{2,1,0:T(8,128)(2,1)S(1)}, bf16[2,128,1024]{2,1,0:T(8,128)(2,1)S(1)}, u32[]{:S(2)}, u32[]{:S(2)}) collective-permute-start(bf16[2,128,1024]{2,1,0:T(8,128)(2,1)S(1)} %get-tuple-element.359), channel_id=1, source_target_pairs={{0,4},{2,6},{4,0},{6,2},{8,12},{10,14},{12,8},{14,10},{16,20},{18,... | collective-permute-start | bytes 1572872 | tf_op jit(solution)/shard_map/ppermute | solution.py:894
  270.6 23.2 %collective-permute-start.9 = (bf16[4,64,1024]{2,1,0:T(8,128)(2,1)S(1)}, bf16[4,64,1024]{2,1,0:T(8,128)(2,1)S(1)}, u32[]{:S(2)}, u32[]{:S(2)}) collective-permute-start(bf16[4,64,1024]{2,1,0:T(8,128)(2,1)S(1)} %get-tuple-element.358), channel_id=1, source_target_pairs={{0,1},{1,0},{2,3},{3,2},{4,5},{5,4},{6,7},{7,6},{8,9},{9,8},{10,11... | collective-permute-start | bytes 1572872 | tf_op jit(solution)/shard_map/ppermute | solution.py:890
  271.1 28.8 %collective-permute-start.8 = (bf16[2,256,1024]{2,1,0:T(8,128)(2,1)S(1)}, bf16[2,256,1024]{2,1,0:T(8,128)(2,1)S(1)}, u32[]{:S(2)}, u32[]{:S(2)}) collective-permute-start(bf16[2,256,1024]{2,1,0:T(8,128)(2,1)S(1)} %get-tuple-element.357), channel_id=1, source_target_pairs={{0,8},{2,10},{4,12},{6,14},{8,0},{10,2},{12,4},{14,6},{16,24},{18,... | collective-permute-start | bytes 3145736 | tf_op jit(solution)/shard_map/ppermute | solution.py:894
  299.9 65.7 %all-to-all-start.3 = ((bf16[16,608,128]{2,1,0:T(8,128)(2,1)}), bf16[16,608,128]{2,1,0:T(8,128)(2,1)}, u32[]{:S(2)}, u32[]{:S(2)}) async-start(bf16[16,608,128]{2,1,0:T(8,128)(2,1)} %attend_back_last.1.refs_0_), calls=%async_computation.3 | async-start | bytes 4980736 | tf_op jit(solution)/shard_map/all_to_all | solution.py:1139
  309.4 13.6 %copy-start.39 = (f32[1,1024]{1,0:T(1,128)S(1)}, f32[1,1024]{1,0:T(1,128)}, u32[]{:S(2)}) copy-start(f32[1,1024]{1,0:T(1,128)} %get-tuple-element.389) | copy-start | bytes 12292
  309.4 14.3 %copy-start.36 = (f32[1,4096]{1,0:T(1,128)S(1)}, f32[1,4096]{1,0:T(1,128)}, u32[]{:S(2)}) copy-start(f32[1,4096]{1,0:T(1,128)} %get-tuple-element.388) | copy-start | bytes 49156
  314.6 21.6 %collective-permute-start.12 = (bf16[2,128,1024]{2,1,0:T(8,128)(2,1)S(1)}, bf16[2,128,1024]{2,1,0:T(8,128)(2,1)S(1)}, u32[]{:S(2)}, u32[]{:S(2)}) collective-permute-start(bf16[2,128,1024]{2,1,0:T(8,128)(2,1)S(1)} %get-tuple-element.372), channel_id=1, source_target_pairs={{0,1},{1,0},{2,3},{3,2},{4,5},{5,4},{6,7},{7,6},{8,9},{9,8},{10,11... | collective-permute-start | bytes 1572872 | tf_op jit(solution)/shard_map/ppermute | solution.py:890
  316.1 20.1 %collective-permute-start.13 = (bf16[2,64,1024]{2,1,0:T(8,128)(2,1)}, bf16[2,64,1024]{2,1,0:T(8,128)(2,1)S(1)}, u32[]{:S(2)}, u32[]{:S(2)}) collective-permute-start(bf16[2,64,1024]{2,1,0:T(8,128)(2,1)} %get-tuple-element.373), channel_id=1, source_target_pairs={{0,4},{2,6},{4,0},{6,2},{8,12},{10,14},{12,8},{14,10},{16,20},{18,... | collective-permute-start | bytes 786440 | tf_op jit(solution)/shard_map/ppermute | solution.py:894
  317.9 18.4 %collective-permute-start.14 = (bf16[2,64,1024]{2,1,0:T(8,128)(2,1)S(1)}, bf16[2,64,1024]{2,1,0:T(8,128)(2,1)S(1)}, u32[]{:S(2)}, u32[]{:S(2)}) collective-permute-start(bf16[2,64,1024]{2,1,0:T(8,128)(2,1)S(1)} %get-tuple-element.374), channel_id=1, source_target_pairs={{0,1},{1,0},{2,3},{3,2},{4,5},{5,4},{6,7},{7,6},{8,9},{9,8},{10,11... | collective-permute-start | bytes 786440 | tf_op jit(solution)/shard_map/ppermute | solution.py:890
  318.4 17.9 %collective-permute-start.15 = (bf16[2,32,1024]{2,1,0:T(8,128)(2,1)}, bf16[2,32,1024]{2,1,0:T(8,128)(2,1)S(1)}, u32[]{:S(2)}, u32[]{:S(2)}) collective-permute-start(bf16[2,32,1024]{2,1,0:T(8,128)(2,1)} %copy-done.16), channel_id=1, source_target_pairs={{0,4},{2,6},{4,0},{6,2},{8,12},{10,14},{12,8},{14,10},{16,20},{18,... | collective-permute-start | bytes 393224 | tf_op jit(solution)/shard_map/ppermute | solution.py:894
  338.0 15.5 %copy-start.38 = (f32[1024]{0:T(1024)S(1)}, f32[1024]{0:T(1024)}, u32[]{:S(2)}) copy-start(f32[1024]{0:T(1024)} %param.69) | copy-start | bytes 12292
  338.0 15.6 %copy-start.37 = (f32[1024]{0:T(1024)S(1)}, f32[1024]{0:T(1024)}, u32[]{:S(2)}) copy-start(f32[1024]{0:T(1024)} %param.70) | copy-start | bytes 12292
  338.2 25.8 %copy-start.18 = (bf16[2,128,1024]{2,1,0:T(8,128)(2,1)S(1)}, bf16[2,128,1024]{2,1,0:T(8,128)(2,1)}, u32[]{:S(2)}) copy-start(bf16[2,128,1024]{2,1,0:T(8,128)(2,1)} %copy-done.17) | copy-start | bytes 1572868
  338.2 25.8 %copy-start.20 = (bf16[2,64,1024]{2,1,0:T(8,128)(2,1)S(1)}, bf16[2,64,1024]{2,1,0:T(8,128)(2,1)}, u32[]{:S(2)}) copy-start(bf16[2,64,1024]{2,1,0:T(8,128)(2,1)} %copy-done.19) | copy-start | bytes 786436
  338.2 25.8 %copy-start.22 = (bf16[2,64,1024]{2,1,0:T(8,128)(2,1)S(1)}, bf16[2,64,1024]{2,1,0:T(8,128)(2,1)}, u32[]{:S(2)}) copy-start(bf16[2,64,1024]{2,1,0:T(8,128)(2,1)} %copy-done.21) | copy-start | bytes 786436
  338.2 25.8 %copy-start.24 = (bf16[2,32,1024]{2,1,0:T(8,128)(2,1)S(1)}, bf16[2,32,1024]{2,1,0:T(8,128)(2,1)}, u32[]{:S(2)}) copy-start(bf16[2,32,1024]{2,1,0:T(8,128)(2,1)} %copy-done.23) | copy-start | bytes 393220
  341.8 8.0 %collective-permute-start.16 = (bf16[16,32,256]{2,1,0:T(8,128)(2,1)S(1)}, bf16[16,32,256]{2,1,0:T(8,128)(2,1)S(1)}, u32[]{:S(2)}, u32[]{:S(2)}) collective-permute-start(bf16[16,32,256]{2,1,0:T(8,128)(2,1)S(1)} %fusion.1), channel_id=1, source_target_pairs={{0,1},{1,0},{2,3},{3,2},{4,5},{5,4},{6,7},{7,6},{8,9},{9,8},{10,11... | collective-permute-start | bytes 786440 | tf_op jit(solution)/shard_map/ppermute | solution.py:1158
  350.9 2.8 collective-permute-start.17
  351.0 5.1 %collective-permute-start.18 = (bf16[4,32,256]{2,1,0:T(8,128)(2,1)S(1)}, bf16[4,32,256]{2,1,0:T(8,128)(2,1)S(1)}, u32[]{:S(2)}, u32[]{:S(2)}) collective-permute-start(bf16[4,32,256]{2,1,0:T(8,128)(2,1)S(1)} %get-tuple-element.438), channel_id=1, source_target_pairs={{0,4},{2,6},{4,0},{6,2},{8,12},{10,14},{12,8},{14,10},{16,20},{18,... | collective-permute-start | bytes 196616 | tf_op jit(solution)/shard_map/ppermute | solution.py:898
  353.4 4.0 %collective-permute-start.19 = (bf16[4,32,256]{2,1,0:T(8,128)(2,1)S(1)}, bf16[4,32,256]{2,1,0:T(8,128)(2,1)S(1)}, u32[]{:S(2)}, u32[]{:S(2)}) collective-permute-start(bf16[4,32,256]{2,1,0:T(8,128)(2,1)S(1)} %get-tuple-element.437), channel_id=1, source_target_pairs={{0,6},{2,4},{4,2},{6,0},{8,14},{10,12},{12,10},{14,8},{16,22},{18,... | collective-permute-start | bytes 196616 | tf_op jit(solution)/shard_map/ppermute | solution.py:898
  358.2 9.4 %collective-permute-start.20 = (bf16[4,32,256]{2,1,0:T(8,128)(2,1)}, bf16[4,32,256]{2,1,0:T(8,128)(2,1)}, u32[]{:S(2)}, u32[]{:S(2)}) collective-permute-start(bf16[4,32,256]{2,1,0:T(8,128)(2,1)} %get-tuple-element.435), channel_id=1, source_target_pairs={{0,8},{2,10},{4,12},{6,14},{8,0},{10,2},{12,4},{14,6},{16,24},{18,... | collective-permute-start | bytes 196616 | tf_op jit(solution)/shard_map/ppermute | solution.py:898
  361.7 7.7 %collective-permute-start.21 = (bf16[4,32,256]{2,1,0:T(8,128)(2,1)}, bf16[4,32,256]{2,1,0:T(8,128)(2,1)}, u32[]{:S(2)}, u32[]{:S(2)}) collective-permute-start(bf16[4,32,256]{2,1,0:T(8,128)(2,1)} %get-tuple-element.434), channel_id=1, source_target_pairs={{0,16},{2,18},{4,20},{6,22},{8,24},{10,26},{12,28},{14,30},{16,0},... | collective-permute-start | bytes 196616 | tf_op jit(solution)/shard_map/ppermute | solution.py:898
  361.7 8.8 %collective-permute-start.22 = (bf16[4,32,256]{2,1,0:T(8,128)(2,1)}, bf16[4,32,256]{2,1,0:T(8,128)(2,1)}, u32[]{:S(2)}, u32[]{:S(2)}) collective-permute-start(bf16[4,32,256]{2,1,0:T(8,128)(2,1)} %get-tuple-element.433), channel_id=1, source_target_pairs={{0,24},{2,26},{4,28},{6,30},{8,16},{10,18},{12,20},{14,22},{16,8},... | collective-permute-start | bytes 196616 | tf_op jit(solution)/shard_map/ppermute | solution.py:898
  365.5 14.8 %collective-permute-start.26 = (bf16[1,32,1024]{2,1,0:T(8,128)(2,1)S(1)}, bf16[1,32,1024]{2,1,0:T(8,128)(2,1)S(1)}, u32[]{:S(2)}, u32[]{:S(2)}) collective-permute-start(bf16[1,32,1024]{2,1,0:T(8,128)(2,1)S(1)} %get-tuple-element.406), channel_id=1, source_target_pairs={{0,8},{2,10},{4,12},{6,14},{8,0},{10,2},{12,4},{14,6},{16,24},{18,... | collective-permute-start | bytes 196616 | tf_op jit(solution)/shard_map/ppermute | solution.py:894
  366.7 15.3 %collective-permute-start.25 = (bf16[1,64,1024]{2,1,0:T(8,128)(2,1)S(1)}, bf16[1,64,1024]{2,1,0:T(8,128)(2,1)S(1)}, u32[]{:S(2)}, u32[]{:S(2)}) collective-permute-start(bf16[1,64,1024]{2,1,0:T(8,128)(2,1)S(1)} %get-tuple-element.405), channel_id=1, source_target_pairs={{0,16},{2,18},{4,20},{6,22},{8,24},{10,26},{12,28},{14,30},{16,0},... | collective-permute-start | bytes 393224 | tf_op jit(solution)/shard_map/ppermute | solution.py:894
  367.6 14.4 %collective-permute-start.24 = (bf16[1,64,1024]{2,1,0:T(8,128)(2,1)S(1)}, bf16[1,64,1024]{2,1,0:T(8,128)(2,1)S(1)}, u32[]{:S(2)}, u32[]{:S(2)}) collective-permute-start(bf16[1,64,1024]{2,1,0:T(8,128)(2,1)S(1)} %get-tuple-element.404), channel_id=1, source_target_pairs={{0,8},{2,10},{4,12},{6,14},{8,0},{10,2},{12,4},{14,6},{16,24},{18,... | collective-permute-start | bytes 393224 | tf_op jit(solution)/shard_map/ppermute | solution.py:894
  369.4 18.0 %collective-permute-start.23 = (bf16[1,128,1024]{2,1,0:T(8,128)(2,1)S(1)}, bf16[1,128,1024]{2,1,0:T(8,128)(2,1)S(1)}, u32[]{:S(2)}, u32[]{:S(2)}) collective-permute-start(bf16[1,128,1024]{2,1,0:T(8,128)(2,1)S(1)} %get-tuple-element.403), channel_id=1, source_target_pairs={{0,16},{2,18},{4,20},{6,22},{8,24},{10,26},{12,28},{14,30},{16,0},... | collective-permute-start | bytes 786440 | tf_op jit(solution)/shard_map/ppermute | solution.py:894
  371.4 16.0 %copy-start.26 = (bf16[1,64,1024]{2,1,0:T(8,128)(2,1)S(1)}, bf16[1,64,1024]{2,1,0:T(8,128)(2,1)}, u32[]{:S(2)}) copy-start(bf16[1,64,1024]{2,1,0:T(8,128)(2,1)} %copy-done.25) | copy-start | bytes 393220
  (27 other events, 82.4 us)
Sparse Core Ops, SparseCore 0:
  86.0 86.0 all-gather.2
where the time goes:
time: 404 us; the launch traced here: 399 us
  Pallas kernels  169 us (42%)
  blocking collectives  63.6 us (16%)
  waiting for transfers between devices  63.2 us (16%)
  starting transfers between devices  38.4 us (10%)
  local copies, waits for them, and re-layouts  30.3 us (8%)
  between operations  15.3 us (4%)
  other arithmetic  14.4 us (4%)
  matrix products  4.41 us (1%)
    all_to_all x1, blocking collectives, exchange(): return lax.all_to_all(message, 'seq', 0, 0, tiled=True)  63.6 us
    pallas_call x1, Pallas kernels, attend_back_first(): pl.pallas_call(lambda *refs: back_first_kernel(sz, *refs), in_specs=[smem...  37.5 us
    pallas_call x1, Pallas kernels, attend(): pl.pallas_call(lambda *refs: attend_kernel(sz, *refs), in_specs=[smem, sm...  28.5 us
    pallas_call x1, Pallas kernels, feed(): pl.pallas_call(lambda *refs: feed_kernel(sz, *refs), grid=(steps,), in_sp...  26.9 us
    all_to_all x1, waiting for transfers between devices, per_device(): heads_in = lax.all_to_all(out_message, 'seq', 0, 0, tiled=True)[::sz.rep]  25.7 us
    unnamed x90, local copies, waits for them, and re-layouts  20.3 us
    pallas_call x1, Pallas kernels, attend_back_last(): pl.pallas_call(lambda *refs: back_last_kernel(sz, *refs), in_specs=[smem,...  20.2 us
    pallas_call x1, Pallas kernels, weights(): pl.pallas_call(lambda *refs: weights_kernel(sz, *refs), grid=(steps,), in...  18.3 us
  transfers between devices with their start and end apart: 31, of which 12 were waited for; matrix products, arithmetic and copies ran while one was open for 6% of the time, Pallas kernels for 39%

commit v1 on v0

--- a/solution.py
+++ b/solution.py
@@ -1,5 +1,6 @@
 import jax
 import jax.numpy as jnp
+import numpy as np
 from jax import lax
 from jax.experimental import pallas as pl
 from jax.experimental.pallas import tpu as pltpu
@@ -147,6 +148,7 @@
         self.m = m
         self.heads = width // HEAD_DIM
         self.rep = n // self.heads
+        self.slabs = slabs
         self.shards = n * m
         self.bits = (n // 2).bit_length() - 1
         self.per_unit = CLIP_MIN // slabs
@@ -176,7 +178,39 @@
     return folded
 
 
-def project_kernel(sz, tok, gain, offset, wq, wk, wv, bq, bk, bv, cos, sin, meta, msg, normed_out):
+def turn_table():
+    table = np.zeros((LANES, 2 * LANES), np.float32)
+    for section, (begin_at, count) in enumerate(SECTIONS):
+        frequency = np.power(10000.0, -np.arange(count) / count)
+        for place in range(16):
+            for head in range(LANES // HEAD_DIM):
+                for half in range(2):
+                    at = head * HEAD_DIM + begin_at + half * count
+                    table[16 * section + place, at : at + count] = np.cos(place * frequency)
+                    at = at + LANES
+                    table[16 * section + place, at : at + count] = np.sin(place * frequency)
+    return jnp.asarray(table)
+
+
+def own_turns(sz, facts, table):
+    slabs = sz.slabs
+    per_slab = sz.rows // slabs
+    side = int(round(per_slab**0.5))
+    row = lax.broadcasted_iota(jnp.int32, (sz.rows, 1), 0)
+    inside = row
+    first = [jnp.full((sz.rows, 1), facts[2 + section]) for section in range(3)]
+    for slab in range(1, slabs):
+        here = row >= slab * per_slab
+        inside = jnp.where(here, row - slab * per_slab, inside)
+        first = [jnp.where(here, facts[2 + 3 * slab + section], first[section]) for section in range(3)]
+    down = jnp.floor((inside.astype(F32) + 0.5) * (1.0 / side)).astype(jnp.int32)
+    lane = lane_index((1, LANES))
+    place = jnp.where(lane < 16, first[0], jnp.where(lane < 32, first[1] + down, first[2] + inside - down * side))
+    hit = jnp.where((place == lane % 16) & (lane < 48), 1.0, 0.0)
+    return jnp.dot(hit, table, precision=lax.Precision.HIGHEST, preferred_element_type=F32)
+
+
+def project_kernel(sz, facts, tok, gain, offset, wq, wk, wv, bq, bk, bv, table, msg, normed_out, turns):
     step = pl.program_id(0)
 
     @pl.when(step == 0)
@@ -185,14 +219,22 @@
         rows = (unit * gain[...] + offset[...]).astype(BF16)
         normed_out[0 : sz.rows, :] = rows
         normed_out[sz.rows :, :] = jnp.zeros((sz.slot - sz.rows, sz.width), BF16)
-
+        turns[...] = own_turns(sz, facts, table[...])
+
+    cos = turns.at[:, 0:LANES]
+    sin = turns.at[:, LANES:]
+    row = lax.broadcasted_iota(jnp.int32, (8, LANES), 0)
+    meta = jnp.zeros((8, LANES), F32)
+    for place in range(8):
+        right = (row == place) & (lane_index((8, LANES)) >= HEAD_DIM)
+        meta = jnp.where(right, facts[place].astype(F32), meta)
     normed = normed_out[0 : sz.rows, :]
     query = dot(normed, wq[...]) + bq[...]
     key = dot(normed, wk[...]) + bk[...]
     value = dot(normed, wv[...]) + bv[...]
     left = lane_index((sz.rows, LANES)) < HEAD_DIM
     spare = sz.slot - sz.rows
-    facts = jnp.concatenate([jnp.zeros((sz.fold - 8, LANES), F32), meta[...]], axis=0)
+    spare_facts = jnp.concatenate([jnp.zeros((sz.fold - 8, LANES), F32), meta], axis=0)
     for pair in range(query.shape[1] // LANES):
         cols = slice(pair * LANES, (pair + 1) * LANES)
         q_pair = rotate_pair(query[:, cols], cos[...], sin[...], False) * 0.125
@@ -201,12 +243,12 @@
         both = (jnp.where(left, k_pair, swap_halves(v_pair)), jnp.where(left, swap_halves(k_pair), v_pair))
         for head in range(2):
             tail = jnp.where(left[:spare], both[head][sz.rows - spare :], 0.0)
-            folded = fold_head(q_pair, sz, head == 1) + facts
+            folded = fold_head(q_pair, sz, head == 1) + spare_facts
             rows = jnp.concatenate([both[head], tail, folded], axis=0)
             msg[2 * pair + head] = rows.astype(BF16)
 
 
-def project(sz, tokens, gain, offset, weight, bias, cos, sin, meta):
+def project(sz, facts, tokens, gain, offset, weight, bias):
     cols = 256
     steps = sz.width // cols
     whole = lambda shape: pl.BlockSpec(shape, lambda j: (0,) * len(shape))
@@ -216,9 +258,10 @@
     return pl.pallas_call(
         lambda *refs: project_kernel(sz, *refs),
         grid=(steps,),
-        in_specs=[whole((sz.rows, sz.width)), whole((1, sz.width)), whole((1, sz.width))]
+        in_specs=[pl.BlockSpec(memory_space=pltpu.SMEM)]
+        + [whole((sz.rows, sz.width)), whole((1, sz.width)), whole((1, sz.width))]
         + [part(0), part(1), part(2), part_bias(0), part_bias(1), part_bias(2)]
-        + [whole((sz.rows, LANES)), whole((sz.rows, LANES)), whole((8, LANES))],
+        + [whole((LANES, 2 * LANES))],
         out_specs=[
             pl.BlockSpec((heads, sz.msg, LANES), lambda j: (j, 0, 0)),
             whole((sz.slot, sz.width)),
@@ -227,10 +270,11 @@
             jax.ShapeDtypeStruct((sz.heads, sz.msg, LANES), BF16),
             jax.ShapeDtypeStruct((sz.slot, sz.width), BF16),
         ],
+        scratch_shapes=[pltpu.VMEM((sz.rows, 2 * LANES), F32)],
         compiler_params=params(),
         cost_estimate=cost(8),
         name="project",
-    )(tokens, gain, offset, weight, weight, weight, bias, bias, bias, cos, sin, meta)
+    )(facts, tokens, gain, offset, weight, weight, weight, bias, bias, bias, turn_table())
 
 
 def unfold_slot(folded, sz, right):
@@ -527,8 +571,8 @@
 
 def feed_kernel(sz, place, tok, heads_in, wo, bo, gain, offset, we, be, wr, br, cot, *refs):
     result, grad_hidden, msg, shared, grad_exp, act_sent, act_own = refs[:7]
-    grad_be, grad_gain, grad_offset, grad_bo, grad_br = refs[7:12]
-    hidden, reduced, grad_normed = refs[12:]
+    small = refs[7]
+    hidden, reduced, grad_normed = refs[8:]
     step = pl.program_id(0)
     core = place[0]
     left = lane_index((sz.fold, LANES)) < HEAD_DIM
@@ -559,7 +603,10 @@
     act_low = activated.astype(BF16)
     reduced[...] += dot(act_low, wr[...])
     grad_expanded = (dot_cols(cot[...], wr[...]) * slope).astype(BF16)
-    grad_be[...] = jnp.sum(grad_expanded.astype(F32), axis=0, keepdims=True)
+    span = act_low.shape[1]
+    per = sz.width // span
+    lanes = pl.ds(pl.multiple_of(lax.rem(step, per) * span, LANES), span)
+    small[pl.ds(4 + step // per, 1), lanes] = jnp.sum(grad_expanded.astype(F32), axis=0, keepdims=True)
     grad_normed[...] += dot_cols(grad_expanded, we[...])
     act_own[...] = core_cols(activated, sz.ff // sz.n, core).astype(BF16)
     act_sent[...] = core_cols(activated, sz.ff // sz.n, 1 - core).astype(BF16)
@@ -573,12 +620,12 @@
         part, gain_part, offset_part = norm_back(grad_normed[...], rows, gain[...])
         total = out_grad + part
         grad_hidden[...] = total
-        grad_gain[...] = gain_part
-        grad_offset[...] = offset_part
-        grad_br[...] = jnp.sum(out_grad, axis=0, keepdims=True)
         low = total.astype(BF16)
+        small[0:1, :] = jnp.sum(low.astype(F32), axis=0, keepdims=True)
+        small[1:2, :] = gain_part
+        small[2:3, :] = offset_part
+        small[3:4, :] = jnp.sum(out_grad, axis=0, keepdims=True)
         shared[:, 2 * sz.width : 3 * sz.width] = low
-        grad_bo[...] = jnp.sum(low.astype(F32), axis=0, keepdims=True)
         for quarter in range(4):
             wide = sz.width // 4
             grad_attended = dot_cols(low, wo[quarter * wide : (quarter + 1) * wide, :])
@@ -595,7 +642,6 @@
     whole = lambda *shape: pl.BlockSpec(shape, lambda j: (0,) * len(shape), pipeline_mode=pl.Buffered(1))
     shape = jax.ShapeDtypeStruct
     vector = whole(1, sz.width)
-    vector_out = shape((1, sz.width), F32)
     return pl.pallas_call(
         lambda *refs: feed_kernel(sz, *refs),
         grid=(steps,),
@@ -621,11 +667,7 @@
             pl.BlockSpec((sz.rows, span), lambda j: (0, j)),
             pl.BlockSpec((sz.rows, span // 2), lambda j: (0, j)),
             pl.BlockSpec((sz.rows, span // 2), lambda j: (0, j)),
-            pl.BlockSpec((1, span), lambda j: (0, j)),
-            vector,
-            vector,
-            vector,
-            vector,
+            whole(4 + sz.ff // sz.width, sz.width),
         ],
         out_shape=[
             shape((sz.rows, sz.width), BF16),
@@ -635,11 +677,7 @@
             shape((sz.rows, sz.ff), BF16),
             shape((sz.rows, sz.ff // 2), BF16),
             shape((sz.rows, sz.ff // 2), BF16),
-            shape((1, sz.ff), F32),
-            vector_out,
-            vector_out,
-            vector_out,
-            vector_out,
+            shape((4 + sz.ff // sz.width, sz.width), F32),
         ],
         scratch_shapes=[pltpu.VMEM((sz.rows, sz.width), F32)] * 3,
         compiler_params=params(),
@@ -848,7 +886,7 @@
             outs += 1
 
 
-def halve(sz, place, sides, labels):
+def halve(sz, place, sides, labels, mib=63):
     parts = [side.split(label) for side, label in zip(sides, labels)]
     grid = 2 if all(before % 2 == 0 for before, _, _ in parts) else 1
     ins, in_specs, out_specs, out_shape = [], [], [], []
@@ -872,7 +910,7 @@
             num_scalar_prefetch=1, grid=(grid,), in_specs=in_specs, out_specs=out_specs
         ),
         out_shape=out_shape,
-        compiler_params=params(sz, 20),
+        compiler_params=params(sz, mib),
         cost_estimate=cost(4),
         name="halve",
     )(place, *ins)
@@ -1032,9 +1070,7 @@
     first_unit = lower[0] // CLIP_MIN
     unit_count = (upper[0] - lower[0]) // CLIP_MIN
     corners = positions[0].reshape(3, slabs, -1)[:, :, 0].T.reshape(-1)
-    meta = jnp.concatenate([jnp.stack([first_unit, unit_count]), corners])[:8, None]
-    meta = jnp.where(jnp.arange(LANES) < HEAD_DIM, 0, meta).astype(F32)
-    cos, sin = lane_tables(positions[0])
+    own_facts = jnp.concatenate([jnp.stack([first_unit, unit_count]), corners]).astype(jnp.int32)
     row = lambda vector: vector.reshape(1, -1)
     me, mine_dp = lax.axis_index("seq"), lax.axis_index("dp")
     place = jnp.stack([me % 2] + [me // (2 << bit) % 2 for bit in range(sz.bits)] + [mine_dp, me * m + mine_dp])
@@ -1052,7 +1088,7 @@
     ]
     head_weight = jnp.concatenate(head_weight + [jnp.zeros((width, HEAD_DIM), BF16)], axis=1)
     message, normed = project(
-        sz, tokens[0], row(first_gain), row(first_offset), triple_weight, row(triple_bias), cos, sin, meta
+        sz, own_facts, tokens[0], row(first_gain), row(first_offset), triple_weight, row(triple_bias)
     )
     recv = exchange(message)
     chips = list(range(0, n // 2, 2)) + list(range(n // 2 - 1, 0, -2))
@@ -1071,16 +1107,12 @@
         grad_exp,
         act_sent,
         act_own,
-        grad_be,
-        grad_second_gain,
-        grad_second_offset,
-        grad_bo,
-        grad_br,
+        small,
     ) = feed(
         sz,
         place,
         tokens[0],
-        after(heads_in, turns),
+        after(heads_in, turns, head_weight),
         output_weight,
         row(output_bias),
         row(second_gain),
@@ -1131,22 +1163,22 @@
         sz, unit_first, unit_span, after(recv_grad, wo_parts[0]), qs, kvs, kept
     )
     add(got, grad_kv)
-    sent = halve(sz, place, sides, rounds[1])
+    sent = halve(sz, place, sides, rounds[1], 20)
     got = move(rounds[1])
     back_message = attend_back_last(
         sz, unit_first, unit_span, after(dos, sent), qs, kvs, kept, grad_q, grad_kv, turns
     )
     back = lax.all_to_all(after(back_message, got), "seq", 0, 0, tiled=True)[:: sz.rep]
     add(got, back_message)
-    sent = halve(sz, place, sides, rounds[2])
+    sent = halve(sz, place, sides, rounds[2], 20)
     got = move(rounds[2])
     head_grad = triple_grad(sz, after(back_message, sent), normed_all)
-    columns = [grad_bo, grad_second_gain, grad_second_offset, grad_be, grad_br]
-    columns = [column.reshape(shards, -1) for column in after(columns, back_message)]
-    spans = [column.shape[1] for column in columns]
+    small = after(small, back_message)
+    small = [small[:4].reshape(4, shards, few).transpose(1, 0, 2).reshape(shards, -1), small[4:].reshape(shards, -1)]
+    small = jnp.concatenate(small, axis=1)
+    spans = [few] * 4 + [fan * few]
+    small = jnp.pad(small, ((0, 0), (0, 4 * HEAD_DIM - small.shape[1]))).reshape(shards, 4, HEAD_DIM)
     head_grad = after(head_grad, got)
-    small = jnp.concatenate(columns, axis=1)
-    small = jnp.pad(small, ((0, 0), (0, 4 * HEAD_DIM - small.shape[1]))).reshape(shards, 4, HEAD_DIM)
     along = jnp.sum(head_grad * head_weight.astype(F32), axis=1).reshape(shards, 1, few)
     along = jnp.pad(along, ((0, 0), (0, 0), (0, HEAD_DIM - few)))
     spare = jnp.concatenate([small, along], axis=1)
@@ -1183,7 +1215,7 @@
     bias_qk = lax.dynamic_slice(bias_all[0], (shard * 2 * few,), (2 * few,))
     bias_v = lax.dynamic_slice(bias_all[0], (2 * width + shard * few,), (few,))
     gain_one, offset_one = gain_one[0], offset_one[0]
-    bias_o, gain_two, offset_two, bias_e, bias_r = [vector[0] for vector in vectors]
+    bias_o, gain_two, offset_two, bias_r, bias_e = [vector[0] for vector in vectors]
     return (
         result[None],
         input_grad[None],

time: 404 us -> 411 us (1.017)
  Pallas kernels: 169 us -> 193 us
  other arithmetic: 14.4 us -> 5.31 us
  waiting for transfers between devices: 63.2 us -> 55.7 us
    pallas_call x1, Pallas kernels: 37.5 us -> 47.8 us  [attend_back_first(): pl.pallas_call(lambda *refs: back_first_kernel(sz, *refs), in_specs=[smem...]
    ppermute x12, waiting for transfers between devices: 17.6 us -> 10.3 us  [send(): lax.ppermute(block, 'seq', [(i, i ^ bit) for i in range(sz.n)])]
    pallas_call x1, Pallas kernels: 28.5 us -> 35 us  [attend(): pl.pallas_call(lambda *refs: attend_kernel(sz, *refs), in_specs=[smem, sm...]
    pallas_call x1, Pallas kernels: 20.2 us -> 24.6 us  [attend_back_last(): pl.pallas_call(lambda *refs: back_last_kernel(sz, *refs), in_specs=[smem,...]
    unnamed x90 -> x98, local copies, waits for them, and re-layouts: 20.3 us -> 24.1 us
  transfers between devices with their start and end apart: 31 -> 31, of which waited for: 12 -> 7; matrix products, arithmetic and copies ran while one was open for 6% -> 4% of each run, Pallas kernels for 39% -> 44%
where the time goes in v1:
time: 411 us; the launch traced here: 407 us
  Pallas kernels  193 us (47%)
  blocking collectives  63.6 us (15%)
  waiting for transfers between devices  55.7 us (14%)
  starting transfers between devices  37.7 us (9%)
  local copies, waits for them, and re-layouts  32.7 us (8%)
  between operations  15.3 us (4%)
  other arithmetic  5.31 us (1%)
  matrix products  4.39 us (1%)
    all_to_all x1, blocking collectives, exchange(): return lax.all_to_all(message, 'seq', 0, 0, tiled=True)  63.6 us
    pallas_call x1, Pallas kernels, attend_back_first(): pl.pallas_call(lambda *refs: back_first_kernel(sz, *refs), in_specs=[smem...  47.8 us
    pallas_call x1, Pallas kernels, attend(): pl.pallas_call(lambda *refs: attend_kernel(sz, *refs), in_specs=[smem, sm...  35 us
    pallas_call x1, Pallas kernels, feed(): pl.pallas_call(lambda *refs: feed_kernel(sz, *refs), grid=(steps,), in_sp...  26.8 us
    pallas_call x1, Pallas kernels, attend_back_last(): pl.pallas_call(lambda *refs: back_last_kernel(sz, *refs), in_specs=[smem,...  24.6 us
    unnamed x98, local copies, waits for them, and re-layouts  24.1 us
    all_to_all x1, waiting for transfers between devices, per_device(): heads_in = lax.all_to_all(out_message, 'seq', 0, 0, tiled=True)[::sz.rep]  23.1 us
    pallas_call x1, Pallas kernels, weights(): pl.pallas_call(lambda *refs: weights_kernel(sz, *refs), grid=(steps,), in...  18.3 us
  transfers between devices with their start and end apart: 31, of which 7 were waited for; matrix products, arithmetic and copies ran while one was open for 4% of the time, Pallas kernels for 44%

profile of v1, /device:TPU:0, one launch (start us, length us, event | category | flops | bytes accessed | tf_op | source)
XLA Modules:
  0.0 407.2 jit_solution(8813377711148899031)
XLA Ops:
  9.7 9.7 %project.1 = (bf16[16,608,128]{2,1,0:T(8,128)(2,1)}, bf16[400,1024]{1,0:T(8,128)(2,1)}) custom-call(s32[8]{0:T(128)} %pad_add_fusion.2.refs_0_, bf16[392,1024]{1,0:T(8,128)(2,1)} %bitcast.240, f32[1,1024]{1,0:T(1,128)} %bitcast.228, f32[1,1024]{1,0:T(1,128)} %bitcast.227, bf16[1024,3072]{1,0:T(8,128)(2,1)} %refs_4_.3, bf16[1024,3072]{1,0:T(8,128)(2,1)} %refs_4_.3, ...), custom_call_target="tpu_custom_call" | custom-call | flops 9200000000 | bytes 1048576 | tf_op jit(solution)/shard_map/project/pallas_call | solution.py:258
  19.4 63.6 %all_to_all.20.refs_2_ = bf16[16,608,128]{2,1,0:T(8,128)(2,1)S(1)} all-to-all(bf16[16,608,128]{2,1,0:T(8,128)(2,1)} %get-tuple-element.274), channel_id=1, replica_groups=mesh['seq'=16,'dp'=2] {'seq'}, dimensions={0} | all-to-all | bytes 4980736 | tf_op jit(solution)/shard_map/all_to_all | solution.py:1082
  85.9 35.0 %attend.1 = (bf16[16,208,128]{2,1,0:T(8,128)(2,1)}, f32[6656,128]{1,0:T(8,128)}, bf16[6656,128]{1,0:T(8,128)(2,1)}, bf16[6400,128]{1,0:T(8,128)(2,1)}) custom-call(s32[8]{0:T(128)} %bitcast.205, s32[8]{0:T(128)} %bitcast.208, bf16[16,608,128]{2,1,0:T(8,128)(2,1)} %copy-done.37), custom_call_target="tpu_custom_call" | custom-call | flops 36800000000 | bytes 1048576 | tf_op jit(solution)/shard_map/attend/pallas_call | solution.py:364
  120.9 4.6 %all-to-all-start.1 = ((bf16[16,208,128]{2,1,0:T(8,128)(2,1)}), bf16[16,208,128]{2,1,0:T(8,128)(2,1)S(1)}, u32[]{:S(2)}, u32[]{:S(2)}) async-start(bf16[16,208,128]{2,1,0:T(8,128)(2,1)} %get-tuple-element.275), calls=%async_computation.1 | async-start | bytes 1703936 | tf_op jit(solution)/shard_map/all_to_all | solution.py:1101
  126.8 2.3 constant_dynamic-slice_fusion.6
  130.4 1.1 reshape.600
  131.6 4.4 %fusion.2.refs_8_ = f32[6400,128]{1,0:T(8,128)} fusion(pred[6400,48]{0,1:T(8,128)(4,1)S(1)} %reshape.600, f32[16,128]{1,0:T(8,128)S(1)} %get-tuple-element.380, f32[16,128]{1,0:T(8,128)S(1)} %get-tuple-element.379, f32[16,128]{1,0:T(8,128)S(1)} %get-tuple-element.378), kind=kOutput, calls=%fused_computation.20 | convolution fusion | flops 471871488 | bytes 3608576 | tf_op jit(solution)/shard_map/dot_general | solution.py:108
  135.9 23.1 %all-to-all-done.1.refs_2_ = bf16[16,208,128]{2,1,0:T(8,128)(2,1)S(1)} async-done(((bf16[16,208,128]{2,1,0:T(8,128)(2,1)}), bf16[16,208,128]{2,1,0:T(8,128)(2,1)S(1)}, u32[]{:S(2)}, u32[]{:S(2)}) %all-to-all-start.1) | async-done | bytes 852000 | tf_op jit(solution)/shard_map/all_to_all | solution.py:1101
  159.1 1.0 copy-done.41
  160.1 26.8 %feed.1 = (bf16[392,1024]{1,0:T(8,128)(2,1)}, f32[392,1024]{1,0:T(8,128)}, bf16[16,208,128]{2,1,0:T(8,128)(2,1)}, bf16[392,3072]{1,0:T(8,128)(2,1)}, bf16[392,40...) custom-call(s32[6]{0:T(128)} %stack.64.refs_0_, ...), custom_call_target="tpu_custom_call" | custom-call | flops 32199999488 | bytes 1048576 | tf_op jit(solution)/shard_map/feed/pallas_call | solution.py:645
  188.0 3.8 all-to-all-start.2
  191.8 8.2 %collective-permute-done.1.refs_4_ = bf16[392,1024]{1,0:T(8,128)(2,1)} collective-permute-done((bf16[392,1024]{1,0:T(8,128)(2,1)}, bf16[392,1024]{1,0:T(8,128)(2,1)}, u32[]{:S(2)}, u32[]{:S(2)}) %collective-permute-start.1) | collective-permute-done | bytes 802848 | tf_op jit(solution)/shard_map/ppermute | solution.py:1077
  200.1 1.4 copy-done.45
  201.4 18.3 %weights.1 = (bf16[4,256,1024]{2,1,0:T(8,128)(2,1)}, bf16[4,256,1024]{2,1,0:T(8,128)(2,1)}, bf16[8,2,32,1024]{3,2,1,0:T(8,128)(2,1)}, bf16[8,2,32,1024]{3,2,1,0:...) custom-call(s32[6]{0:T(128)} %stack.64.refs_0_, ...), custom_call_target="tpu_custom_call" | custom-call | flops 11500000256 | bytes 1048576 | tf_op jit(solution)/shard_map/weights/pallas_call | solution.py:765
  220.0 1.1 collective-permute-start.4
  221.1 2.0 copy-done.31
  223.1 1.5 copy-done.33
  224.5 1.4 copy-done.34
  226.0 47.8 %attend_back_first.1 = (bf16[6656,128]{1,0:T(8,128)(2,1)S(1)}, f32[6656,128]{1,0:T(8,128)S(1)}, f32[6400,128]{1,0:T(8,128)S(1)}) custom-call(s32[8]{0:T(128)S(1)} %bitcast.206, s32[8]{0:T(128)S(1)} %bitcast.209, bf16[16,208,128]{2,1,0:T(8,128)(2,1)S(1)} %all-to-all-done.2.refs_2_, bf16[6656,128]{1,0:T(8,128)(2,1)S(1)} %copy-done.33, ...), custom_call_target="tpu_custom_call" | custom-call | flops 46000001024 | bytes 1048576 | tf_op jit(solution)/shard_map/attend_back_first/pallas_call | solution.py:466
  274.0 1.6 halve.3
  277.9 1.8 collective-permute-start.11
  279.7 2.0 collective-permute-start.10
  281.7 1.9 collective-permute-start.8
  283.7 24.6 %attend_back_last.1.refs_0_ = bf16[16,608,128]{2,1,0:T(8,128)(2,1)} custom-call(s32[8]{0:T(128)S(1)} %bitcast.207, s32[8]{0:T(128)S(1)} %bitcast.210, bf16[6656,128]{1,0:T(8,128)(2,1)S(1)} %get-tuple-element.305.refs_2_, bf16[6656,128]{1,0:T(8,128)(2,1)S(1)} %copy-done.33, bf16[6400,128]{1,0:T(8,128)(2,1)S(1)} %copy-done.35, f32[6656,128]{1,0:T(8,128)S(1)} %copy-done.32, ...), custom_call_target="tpu_custom_call" | custom-call | flops 23000000512 | bytes 1048576 | tf_op jit(solution)/shard_map/attend_back_last/pallas_call | solution.py:486
  310.6 4.5 %all-to-all-start.3 = ((bf16[16,608,128]{2,1,0:T(8,128)(2,1)}), bf16[16,608,128]{2,1,0:T(8,128)(2,1)}, u32[]{:S(2)}, u32[]{:S(2)}) async-start(bf16[16,608,128]{2,1,0:T(8,128)(2,1)} %attend_back_last.1.refs_0_), calls=%async_computation.3 | async-start | bytes 4980736 | tf_op jit(solution)/shard_map/all_to_all | solution.py:1171
  315.1 1.0 copy-done.8
  316.1 1.0 copy-done.10
  317.1 1.0 copy-done.12
  318.2 1.0 copy-done.14
  319.2 0.9 copy-done.17
  320.2 0.9 copy-done.19
  321.1 1.2 halve.4
  326.5 1.8 collective-permute-start.13
  328.3 2.0 collective-permute-start.14
  331.0 12.1 %triple_grad.1 = f32[1024,256]{1,0:T(8,128)} custom-call(bf16[16,608,128]{2,1,0:T(8,128)(2,1)} %attend_back_last.1.refs_0_, bf16[16,400,1024]{2,1,0:T(8,128)(2,1)} %bitcast.211), custom_call_target="tpu_custom_call" | custom-call | flops 1150000000 | bytes 1048576 | tf_op jit(solution)/shard_map/triple_grad/pallas_call | solution.py:543
  343.1 3.8 collective-permute-done.15
  347.6 1.9 multiply_reduce_fusion
  350.5 7.6 %collective-permute-done.16 = bf16[16,32,256]{2,1,0:T(8,128)(2,1)S(1)} collective-permute-done((bf16[16,32,256]{2,1,0:T(8,128)(2,1)S(1)}, bf16[16,32,256]{2,1,0:T(8,128)(2,1)S(1)}, u32[]{:S(2)}, u32[]{:S(2)}) %collective-permute-start.16) | collective-permute-done | bytes 262176 | tf_op jit(solution)/shard_map/ppermute | solution.py:1190
  358.3 2.4 collective-permute-start.18
  361.0 5.1 %collective-permute-done.18 = bf16[4,32,256]{2,1,0:T(8,128)(2,1)S(1)} collective-permute-done((bf16[4,32,256]{2,1,0:T(8,128)(2,1)S(1)}, bf16[4,32,256]{2,1,0:T(8,128)(2,1)S(1)}, u32[]{:S(2)}, u32[]{:S(2)}) %collective-permute-start.18) | collective-permute-done | bytes 65568 | tf_op jit(solution)/shard_map/ppermute | solution.py:936
  366.1 1.1 collective-permute-done.19
  367.4 3.5 collective-permute-start.21
  371.8 3.3 halve.5
  375.1 3.5 collective-permute-start.25
  378.7 1.4 collective-permute-start.23
  380.2 8.8 %finish.1 = f32[392,1024]{1,0:T(8,128)} custom-call(bf16[16,608,128]{2,1,0:T(8,128)(2,1)} %all-to-all-done.3.refs_0_, bf16[1024,3072]{1,0:T(8,128)(2,1)} %refs_4_.3, bf16[1024,3072]{1,0:T(8,128)(2,1)} %refs_4_.3, bf16[1024,3072]{1,0:T(8,128)(2,1)} %refs_4_.3, bf16[392,1024]{1,0:T(8,128)(2,1)} %bitcast.242, f32[1,1024]{1,0:T(1,128)} %bitcast.229, ...), custom_call_target="tpu_custom_call" | custom-call | flops 11500000256 | bytes 1048576 | tf_op jit(solution)/shard_map/finish/pallas_call | solution.py:825
  389.1 6.5 %collective-permute-done.23 = bf16[1,128,1024]{2,1,0:T(8,128)(2,1)S(1)} collective-permute-done((bf16[1,128,1024]{2,1,0:T(8,128)(2,1)}, bf16[1,128,1024]{2,1,0:T(8,128)(2,1)S(1)}, u32[]{:S(2)}, u32[]{:S(2)}) %collective-permute-start.23) | collective-permute-done | bytes 262176 | tf_op jit(solution)/shard_map/ppermute | solution.py:932
  395.6 3.4 last.1
  (200 shorter events, 22.8 us)
Async XLA Ops:
  7.2 323.8 %all-gather.3.cloned.1.call-start = ((), (), s32[]{:S(2)}) async-start(), calls=%async_computation.4 | async-start | bytes 13926400 | tf_op jit(solution)/shard_map/all_gather | solution.py:1096
  120.9 38.2 %all-to-all-start.1 = ((bf16[16,208,128]{2,1,0:T(8,128)(2,1)}), bf16[16,208,128]{2,1,0:T(8,128)(2,1)S(1)}, u32[]{:S(2)}, u32[]{:S(2)}) async-start(bf16[16,208,128]{2,1,0:T(8,128)(2,1)} %get-tuple-element.275), calls=%async_computation.1 | async-start | bytes 1703936 | tf_op jit(solution)/shard_map/all_to_all | solution.py:1101
  186.9 13.1 %collective-permute-start.2 = (bf16[392,4096]{1,0:T(8,128)(2,1)}, bf16[392,4096]{1,0:T(8,128)(2,1)}, u32[]{:S(2)}, u32[]{:S(2)}) collective-permute-start(bf16[392,4096]{1,0:T(8,128)(2,1)} %get-tuple-element.281.refs_5_), channel_id=1, source_target_pairs={{0,2},{2,0},{4,6},{6,4},{8,10},{10,8},{12,14},{14,12},{16,18},{18,... | collective-permute-start | bytes 9633800 | tf_op jit(solution)/shard_map/ppermute | solution.py:1077
  187.0 13.1 %collective-permute-start.3 = (bf16[392,3072]{1,0:T(8,128)(2,1)}, bf16[392,3072]{1,0:T(8,128)(2,1)S(1)}, u32[]{:S(2)}, u32[]{:S(2)}) collective-permute-start(bf16[392,3072]{1,0:T(8,128)(2,1)} %get-tuple-element.282.refs_7_.refs_9_.refs_11_), channel_id=1, source_target_pairs={{0,2},{2,0},{4,6},{6,4},{8,10},{10,8},{12,14},{14,12},{16,18},{18,... | collective-permute-start | bytes 7225352 | tf_op jit(solution)/shard_map/ppermute | solution.py:1077
  187.5 12.6 %collective-permute-start = (bf16[392,2048]{1,0:T(8,128)(2,1)}, bf16[392,2048]{1,0:T(8,128)(2,1)}, u32[]{:S(2)}, u32[]{:S(2)}) collective-permute-start(bf16[392,2048]{1,0:T(8,128)(2,1)} %get-tuple-element.280), channel_id=1, source_target_pairs={{0,2},{2,0},{4,6},{6,4},{8,10},{10,8},{12,14},{14,12},{16,18},{18,... | collective-permute-start | bytes 4816904 | tf_op jit(solution)/shard_map/ppermute | solution.py:1077
  187.6 12.5 %collective-permute-start.1 = (bf16[392,1024]{1,0:T(8,128)(2,1)}, bf16[392,1024]{1,0:T(8,128)(2,1)}, u32[]{:S(2)}, u32[]{:S(2)}) collective-permute-start(bf16[392,1024]{1,0:T(8,128)(2,1)} %bitcast.238), channel_id=1, source_target_pairs={{0,2},{2,0},{4,6},{6,4},{8,10},{10,8},{12,14},{14,12},{16,18},{18,... | collective-permute-start | bytes 2408456 | tf_op jit(solution)/shard_map/ppermute | solution.py:1077
  188.0 31.7 %all-to-all-start.2 = ((bf16[16,208,128]{2,1,0:T(8,128)(2,1)}), bf16[16,208,128]{2,1,0:T(8,128)(2,1)S(1)}, u32[]{:S(2)}, u32[]{:S(2)}) async-start(bf16[16,208,128]{2,1,0:T(8,128)(2,1)} %get-tuple-element.278), calls=%async_computation.2 | async-start | bytes 1703936 | tf_op jit(solution)/shard_map/all_to_all | solution.py:1082
  201.4 19.7 %copy-start.29 = (s32[8,1]{0,1:T(1,128)S(1)}, s32[8,1]{0,1:T(1,128)}, u32[]{:S(2)}) copy-start(s32[8,1]{0,1:T(1,128)} %slice.200) | copy-start | bytes 100
  201.4 19.7 %copy-start.30 = (s32[8,1]{0,1:T(1,128)S(1)}, s32[8,1]{0,1:T(1,128)}, u32[]{:S(2)}) copy-start(s32[8,1]{0,1:T(1,128)} %slice.201) | copy-start | bytes 100
  219.8 54.1 %collective-permute-start.7 = (bf16[8,32,1024]{2,1,0:T(8,128)(2,1)}, bf16[8,32,1024]{2,1,0:T(8,128)(2,1)S(1)}, u32[]{:S(2)}, u32[]{:S(2)}) collective-permute-start(bf16[8,32,1024]{2,1,0:T(8,128)(2,1)} %get-tuple-element.299), channel_id=1, source_target_pairs={{0,1},{1,0},{2,3},{3,2},{4,5},{5,4},{6,7},{7,6},{8,9},{9,8},{10,11... | collective-permute-start | bytes 1572872 | tf_op jit(solution)/shard_map/ppermute | solution.py:928
  219.8 54.0 %collective-permute-start.6 = (bf16[8,2,32,1024]{3,2,1,0:T(8,128)(2,1)}, bf16[8,2,32,1024]{3,2,1,0:T(8,128)(2,1)S(1)}, u32[]{:S(2)}, u32[]{:S(2)}) collective-permute-start(bf16[8,2,32,1024]{3,2,1,0:T(8,128)(2,1)} %get-tuple-element.297), channel_id=1, source_target_pairs={{0,8},{2,10},{4,12},{6,14},{8,0},{10,2},{12,4},{14,6},{16,24},{18,... | collective-permute-start | bytes 3145736 | tf_op jit(solution)/shard_map/ppermute | solution.py:932
  219.9 54.0 %collective-permute-start.5 = (bf16[8,2,32,1024]{3,2,1,0:T(8,128)(2,1)}, bf16[8,2,32,1024]{3,2,1,0:T(8,128)(2,1)S(1)}, u32[]{:S(2)}, u32[]{:S(2)}) collective-permute-start(bf16[8,2,32,1024]{3,2,1,0:T(8,128)(2,1)} %get-tuple-element.294), channel_id=1, source_target_pairs={{0,16},{2,18},{4,20},{6,22},{8,24},{10,26},{12,28},{14,30},{16,0},... | collective-permute-start | bytes 3145736 | tf_op jit(solution)/shard_map/ppermute | solution.py:932
  220.0 53.9 %collective-permute-start.4 = (bf16[4,256,1024]{2,1,0:T(8,128)(2,1)}, bf16[4,256,1024]{2,1,0:T(8,128)(2,1)S(1)}, u32[]{:S(2)}, u32[]{:S(2)}) collective-permute-start(bf16[4,256,1024]{2,1,0:T(8,128)(2,1)} %get-tuple-element.290), channel_id=1, source_target_pairs={{0,4},{2,6},{4,0},{6,2},{8,12},{10,14},{12,8},{14,10},{16,20},{18,... | collective-permute-start | bytes 6291464 | tf_op jit(solution)/shard_map/ppermute | solution.py:932
  226.0 47.9 %copy-start = (bf16[4,256,1024]{2,1,0:T(8,128)(2,1)S(1)}, bf16[4,256,1024]{2,1,0:T(8,128)(2,1)}, u32[]{:S(2)}) copy-start(bf16[4,256,1024]{2,1,0:T(8,128)(2,1)} %get-tuple-element.289) | copy-start | bytes 6291460
  226.0 47.9 %copy-start.1 = (bf16[8,2,32,1024]{3,2,1,0:T(8,128)(2,1)S(1)}, bf16[8,2,32,1024]{3,2,1,0:T(8,128)(2,1)}, u32[]{:S(2)}) copy-start(bf16[8,2,32,1024]{3,2,1,0:T(8,128)(2,1)} %get-tuple-element.293) | copy-start | bytes 3145732
  226.0 47.9 %copy-start.2 = (bf16[8,2,32,1024]{3,2,1,0:T(8,128)(2,1)S(1)}, bf16[8,2,32,1024]{3,2,1,0:T(8,128)(2,1)}, u32[]{:S(2)}) copy-start(bf16[8,2,32,1024]{3,2,1,0:T(8,128)(2,1)} %get-tuple-element.296) | copy-start | bytes 3145732
  226.0 47.9 %copy-start.4 = (bf16[8,32,1024]{2,1,0:T(8,128)(2,1)S(1)}, bf16[8,32,1024]{2,1,0:T(8,128)(2,1)}, u32[]{:S(2)}) copy-start(bf16[8,32,1024]{2,1,0:T(8,128)(2,1)} %get-tuple-element.283) | copy-start | bytes 1572868
  226.0 47.9 %copy-start.5 = (s32[6]{0:T(128)S(1)}, s32[6]{0:T(128)}, u32[]{:S(2)}) copy-start(s32[6]{0:T(128)} %stack.64.refs_0_) | copy-start | bytes 76
  277.9 30.4 %collective-permute-start.11 = (bf16[1,128,1024]{2,1,0:T(8,128)(2,1)S(1)}, bf16[1,128,1024]{2,1,0:T(8,128)(2,1)S(1)}, u32[]{:S(2)}, u32[]{:S(2)}) collective-permute-start(bf16[1,128,1024]{2,1,0:T(8,128)(2,1)S(1)} %get-tuple-element.304), channel_id=1, source_target_pairs={{0,16},{2,18},{4,20},{6,22},{8,24},{10,26},{12,28},{14,30},{16,0},... | collective-permute-start | bytes 786440 | tf_op jit(solution)/shard_map/ppermute | solution.py:932
  279.7 29.3 %collective-permute-start.10 = (bf16[2,128,1024]{2,1,0:T(8,128)(2,1)S(1)}, bf16[2,128,1024]{2,1,0:T(8,128)(2,1)S(1)}, u32[]{:S(2)}, u32[]{:S(2)}) collective-permute-start(bf16[2,128,1024]{2,1,0:T(8,128)(2,1)S(1)} %get-tuple-element.303), channel_id=1, source_target_pairs={{0,4},{2,6},{4,0},{6,2},{8,12},{10,14},{12,8},{14,10},{16,20},{18,... | collective-permute-start | bytes 1572872 | tf_op jit(solution)/shard_map/ppermute | solution.py:932
  281.7 28.1 %collective-permute-start.9 = (bf16[4,64,1024]{2,1,0:T(8,128)(2,1)S(1)}, bf16[4,64,1024]{2,1,0:T(8,128)(2,1)S(1)}, u32[]{:S(2)}, u32[]{:S(2)}) collective-permute-start(bf16[4,64,1024]{2,1,0:T(8,128)(2,1)S(1)} %get-tuple-element.302), channel_id=1, source_target_pairs={{0,1},{1,0},{2,3},{3,2},{4,5},{5,4},{6,7},{7,6},{8,9},{9,8},{10,11... | collective-permute-start | bytes 1572872 | tf_op jit(solution)/shard_map/ppermute | solution.py:928
  281.7 28.9 %collective-permute-start.8 = (bf16[2,256,1024]{2,1,0:T(8,128)(2,1)S(1)}, bf16[2,256,1024]{2,1,0:T(8,128)(2,1)S(1)}, u32[]{:S(2)}, u32[]{:S(2)}) collective-permute-start(bf16[2,256,1024]{2,1,0:T(8,128)(2,1)S(1)} %get-tuple-element.301), channel_id=1, source_target_pairs={{0,8},{2,10},{4,12},{6,14},{8,0},{10,2},{12,4},{14,6},{16,24},{18,... | collective-permute-start | bytes 3145736 | tf_op jit(solution)/shard_map/ppermute | solution.py:932
  310.6 64.5 %all-to-all-start.3 = ((bf16[16,608,128]{2,1,0:T(8,128)(2,1)}), bf16[16,608,128]{2,1,0:T(8,128)(2,1)}, u32[]{:S(2)}, u32[]{:S(2)}) async-start(bf16[16,608,128]{2,1,0:T(8,128)(2,1)} %attend_back_last.1.refs_0_), calls=%async_computation.3 | async-start | bytes 4980736 | tf_op jit(solution)/shard_map/all_to_all | solution.py:1171
  326.5 20.4 %collective-permute-start.12 = (bf16[2,128,1024]{2,1,0:T(8,128)(2,1)S(1)}, bf16[2,128,1024]{2,1,0:T(8,128)(2,1)S(1)}, u32[]{:S(2)}, u32[]{:S(2)}) collective-permute-start(bf16[2,128,1024]{2,1,0:T(8,128)(2,1)S(1)} %get-tuple-element.316), channel_id=1, source_target_pairs={{0,1},{1,0},{2,3},{3,2},{4,5},{5,4},{6,7},{7,6},{8,9},{9,8},{10,11... | collective-permute-start | bytes 1572872 | tf_op jit(solution)/shard_map/ppermute | solution.py:928
  326.5 20.4 %collective-permute-start.13 = (bf16[2,64,1024]{2,1,0:T(8,128)(2,1)}, bf16[2,64,1024]{2,1,0:T(8,128)(2,1)}, u32[]{:S(2)}, u32[]{:S(2)}) collective-permute-start(bf16[2,64,1024]{2,1,0:T(8,128)(2,1)} %copy-done.15), channel_id=1, source_target_pairs={{0,4},{2,6},{4,0},{6,2},{8,12},{10,14},{12,8},{14,10},{16,20},{18,... | collective-permute-start | bytes 786440 | tf_op jit(solution)/shard_map/ppermute | solution.py:932
  328.3 18.7 %collective-permute-start.14 = (bf16[2,64,1024]{2,1,0:T(8,128)(2,1)S(1)}, bf16[2,64,1024]{2,1,0:T(8,128)(2,1)}, u32[]{:S(2)}, u32[]{:S(2)}) collective-permute-start(bf16[2,64,1024]{2,1,0:T(8,128)(2,1)S(1)} %get-tuple-element.318), channel_id=1, source_target_pairs={{0,1},{1,0},{2,3},{3,2},{4,5},{5,4},{6,7},{7,6},{8,9},{9,8},{10,11... | collective-permute-start | bytes 786440 | tf_op jit(solution)/shard_map/ppermute | solution.py:928
  330.3 16.6 %collective-permute-start.15 = (bf16[2,32,1024]{2,1,0:T(8,128)(2,1)}, bf16[2,32,1024]{2,1,0:T(8,128)(2,1)S(1)}, u32[]{:S(2)}, u32[]{:S(2)}) collective-permute-start(bf16[2,32,1024]{2,1,0:T(8,128)(2,1)} %copy-done.20), channel_id=1, source_target_pairs={{0,4},{2,6},{4,0},{6,2},{8,12},{10,14},{12,8},{14,10},{16,20},{18,... | collective-permute-start | bytes 393224 | tf_op jit(solution)/shard_map/ppermute | solution.py:932
  330.9 16.6 %copy-start.38 = (bf16[1024,64]{1,0:T(8,128)(2,1)S(1)}, bf16[1024,64]{1,0:T(8,128)(2,1)}, u32[]{:S(2)}) copy-start(bf16[1024,64]{1,0:T(8,128)(2,1)} %get-tuple-element.365) | copy-start | bytes 393220
  331.0 16.6 %copy-start.39 = (bf16[1024,64]{1,0:T(8,128)(2,1)S(1)}, bf16[1024,64]{1,0:T(8,128)(2,1)}, u32[]{:S(2)}) copy-start(bf16[1024,64]{1,0:T(8,128)(2,1)} %get-tuple-element.366) | copy-start | bytes 393220
  331.0 16.6 %copy-start.40 = (bf16[1024,64]{1,0:T(8,128)(2,1)S(1)}, bf16[1024,64]{1,0:T(8,128)(2,1)}, u32[]{:S(2)}) copy-start(bf16[1024,64]{1,0:T(8,128)(2,1)} %get-tuple-element.367) | copy-start | bytes 393220
  349.5 11.2 %copy-start.44 = (f32[1024]{0:T(1024)S(1)}, f32[1024]{0:T(1024)}, u32[]{:S(2)}) copy-start(f32[1024]{0:T(1024)} %param.58) | copy-start | bytes 12292
  349.5 11.3 %copy-start.43 = (f32[1024]{0:T(1024)S(1)}, f32[1024]{0:T(1024)}, u32[]{:S(2)}) copy-start(f32[1024]{0:T(1024)} %param.59) | copy-start | bytes 12292
  349.9 8.1 %collective-permute-start.16 = (bf16[16,32,256]{2,1,0:T(8,128)(2,1)S(1)}, bf16[16,32,256]{2,1,0:T(8,128)(2,1)S(1)}, u32[]{:S(2)}, u32[]{:S(2)}) collective-permute-start(bf16[16,32,256]{2,1,0:T(8,128)(2,1)S(1)} %fusion.1), channel_id=1, source_target_pairs={{0,1},{1,0},{2,3},{3,2},{4,5},{5,4},{6,7},{7,6},{8,9},{9,8},{10,11... | collective-permute-start | bytes 786440 | tf_op jit(solution)/shard_map/ppermute | solution.py:1190
  358.2 2.8 collective-permute-start.17
  358.3 7.8 %collective-permute-start.18 = (bf16[4,32,256]{2,1,0:T(8,128)(2,1)S(1)}, bf16[4,32,256]{2,1,0:T(8,128)(2,1)S(1)}, u32[]{:S(2)}, u32[]{:S(2)}) collective-permute-start(bf16[4,32,256]{2,1,0:T(8,128)(2,1)S(1)} %get-tuple-element.374), channel_id=1, source_target_pairs={{0,4},{2,6},{4,0},{6,2},{8,12},{10,14},{12,8},{14,10},{16,20},{18,... | collective-permute-start | bytes 196616 | tf_op jit(solution)/shard_map/ppermute | solution.py:936
  360.7 6.6 %collective-permute-start.19 = (bf16[4,32,256]{2,1,0:T(8,128)(2,1)S(1)}, bf16[4,32,256]{2,1,0:T(8,128)(2,1)S(1)}, u32[]{:S(2)}, u32[]{:S(2)}) collective-permute-start(bf16[4,32,256]{2,1,0:T(8,128)(2,1)S(1)} %get-tuple-element.373), channel_id=1, source_target_pairs={{0,6},{2,4},{4,2},{6,0},{8,14},{10,12},{12,10},{14,8},{16,22},{18,... | collective-permute-start | bytes 196616 | tf_op jit(solution)/shard_map/ppermute | solution.py:936
  367.3 11.3 %collective-permute-start.20 = (bf16[4,32,256]{2,1,0:T(8,128)(2,1)S(1)}, bf16[4,32,256]{2,1,0:T(8,128)(2,1)S(1)}, u32[]{:S(2)}, u32[]{:S(2)}) collective-permute-start(bf16[4,32,256]{2,1,0:T(8,128)(2,1)S(1)} %get-tuple-element.371), channel_id=1, source_target_pairs={{0,8},{2,10},{4,12},{6,14},{8,0},{10,2},{12,4},{14,6},{16,24},{18,... | collective-permute-start | bytes 196616 | tf_op jit(solution)/shard_map/ppermute | solution.py:936
  367.4 11.3 %collective-permute-start.21 = (bf16[4,32,256]{2,1,0:T(8,128)(2,1)S(1)}, bf16[4,32,256]{2,1,0:T(8,128)(2,1)S(1)}, u32[]{:S(2)}, u32[]{:S(2)}) collective-permute-start(bf16[4,32,256]{2,1,0:T(8,128)(2,1)S(1)} %get-tuple-element.370), channel_id=1, source_target_pairs={{0,16},{2,18},{4,20},{6,22},{8,24},{10,26},{12,28},{14,30},{16,0},... | collective-permute-start | bytes 196616 | tf_op jit(solution)/shard_map/ppermute | solution.py:936
  370.9 9.2 %collective-permute-start.22 = (bf16[4,32,256]{2,1,0:T(8,128)(2,1)S(1)}, bf16[4,32,256]{2,1,0:T(8,128)(2,1)S(1)}, u32[]{:S(2)}, u32[]{:S(2)}) collective-permute-start(bf16[4,32,256]{2,1,0:T(8,128)(2,1)S(1)} %get-tuple-element.369), channel_id=1, source_target_pairs={{0,24},{2,26},{4,28},{6,30},{8,16},{10,18},{12,20},{14,22},{16,8},... | collective-permute-start | bytes 196616 | tf_op jit(solution)/shard_map/ppermute | solution.py:936
  375.1 14.0 %collective-permute-start.26 = (bf16[1,32,1024]{2,1,0:T(8,128)(2,1)}, bf16[1,32,1024]{2,1,0:T(8,128)(2,1)S(1)}, u32[]{:S(2)}, u32[]{:S(2)}) collective-permute-start(bf16[1,32,1024]{2,1,0:T(8,128)(2,1)} %get-tuple-element.342), channel_id=1, source_target_pairs={{0,8},{2,10},{4,12},{6,14},{8,0},{10,2},{12,4},{14,6},{16,24},{18,... | collective-permute-start | bytes 196616 | tf_op jit(solution)/shard_map/ppermute | solution.py:932
  375.1 13.9 %collective-permute-start.25 = (bf16[1,64,1024]{2,1,0:T(8,128)(2,1)}, bf16[1,64,1024]{2,1,0:T(8,128)(2,1)S(1)}, u32[]{:S(2)}, u32[]{:S(2)}) collective-permute-start(bf16[1,64,1024]{2,1,0:T(8,128)(2,1)} %get-tuple-element.341), channel_id=1, source_target_pairs={{0,16},{2,18},{4,20},{6,22},{8,24},{10,26},{12,28},{14,30},{16,0},... | collective-permute-start | bytes 393224 | tf_op jit(solution)/shard_map/ppermute | solution.py:932
  378.6 10.4 %collective-permute-start.24 = (bf16[1,64,1024]{2,1,0:T(8,128)(2,1)}, bf16[1,64,1024]{2,1,0:T(8,128)(2,1)S(1)}, u32[]{:S(2)}, u32[]{:S(2)}) collective-permute-start(bf16[1,64,1024]{2,1,0:T(8,128)(2,1)} %get-tuple-element.340), channel_id=1, source_target_pairs={{0,8},{2,10},{4,12},{6,14},{8,0},{10,2},{12,4},{14,6},{16,24},{18,... | collective-permute-start | bytes 393224 | tf_op jit(solution)/shard_map/ppermute | solution.py:932
  378.7 16.8 %collective-permute-start.23 = (bf16[1,128,1024]{2,1,0:T(8,128)(2,1)}, bf16[1,128,1024]{2,1,0:T(8,128)(2,1)S(1)}, u32[]{:S(2)}, u32[]{:S(2)}) collective-permute-start(bf16[1,128,1024]{2,1,0:T(8,128)(2,1)} %get-tuple-element.339), channel_id=1, source_target_pairs={{0,16},{2,18},{4,20},{6,22},{8,24},{10,26},{12,28},{14,30},{16,0},... | collective-permute-start | bytes 786440 | tf_op jit(solution)/shard_map/ppermute | solution.py:932
  380.1 15.4 %copy-start.6 = (s32[6]{0:T(128)S(1)}, s32[6]{0:T(128)}, u32[]{:S(2)}) copy-start(s32[6]{0:T(128)} %stack.64.refs_0_) | copy-start | bytes 76
  380.1 15.4 %copy-start.24 = (bf16[1,128,1024]{2,1,0:T(8,128)(2,1)S(1)}, bf16[1,128,1024]{2,1,0:T(8,128)(2,1)}, u32[]{:S(2)}) copy-start(bf16[1,128,1024]{2,1,0:T(8,128)(2,1)} %get-tuple-element.345) | copy-start | bytes 786436
  380.2 15.4 %copy-start.26 = (bf16[1,64,1024]{2,1,0:T(8,128)(2,1)S(1)}, bf16[1,64,1024]{2,1,0:T(8,128)(2,1)}, u32[]{:S(2)}) copy-start(bf16[1,64,1024]{2,1,0:T(8,128)(2,1)} %get-tuple-element.347) | copy-start | bytes 393220
  380.2 15.4 %copy-start.27 = (bf16[1,64,1024]{2,1,0:T(8,128)(2,1)S(1)}, bf16[1,64,1024]{2,1,0:T(8,128)(2,1)}, u32[]{:S(2)}) copy-start(bf16[1,64,1024]{2,1,0:T(8,128)(2,1)} %get-tuple-element.349) | copy-start | bytes 393220
  380.2 15.4 %copy-start.28 = (bf16[1,32,1024]{2,1,0:T(8,128)(2,1)S(1)}, bf16[1,32,1024]{2,1,0:T(8,128)(2,1)}, u32[]{:S(2)}) copy-start(bf16[1,32,1024]{2,1,0:T(8,128)(2,1)} %get-tuple-element.351) | copy-start | bytes 196612
  (31 other events, 80.1 us)
Sparse Core Ops, SparseCore 0:
  83.2 86.0 all-gather.2

commit v2 on v1

--- a/solution.py
+++ b/solution.py
@@ -295,12 +295,12 @@
     target[pl.ds(at + sz.fold, sz.slot - sz.fold), :] = high
 
 
-def loop(count, body):
+def loop(count, body, unroll=1):
     def step(index, carry):
         body(index)
         return carry
 
-    lax.fori_loop(0, count, step, 0)
+    lax.fori_loop(0, count, step, 0, unroll=unroll)
 
 
 def attend_kernel(sz, first, count, recv, out, kept, qs, kvs, ones_v):
@@ -314,7 +314,7 @@
         one = jnp.where(real, 1.0, 0.0)
         ones_v[pl.ds(at, sz.slot), :] = jnp.where(left, one, kv.astype(F32)).astype(BF16)
 
-    loop(sz.n, unpack)
+    loop(sz.n, unpack, 4)
     qs[sz.tokens :, :] = jnp.zeros((Q_TILE, LANES), BF16)
     kept[sz.tokens :, :] = jnp.zeros((Q_TILE, LANES), F32)
 
@@ -354,7 +354,7 @@
         left = lane_index((sz.slot - sz.rows, LANES)) < HEAD_DIM
         kept[pl.ds(at + sz.rows, sz.slot - sz.rows), :] = jnp.where(left, MASKED, 0.0)
 
-    loop(sz.n, pack)
+    loop(sz.n, pack, 4)
 
 
 def attend(sz, first, count, recv):
@@ -429,7 +429,7 @@
         unfold_into(dos, at, recv_grad[src], sz, True)
         grad_kv[pl.ds(at, sz.slot), :] = jnp.zeros((sz.slot, LANES), F32)
 
-    loop(sz.n, unpack)
+    loop(sz.n, unpack, 4)
     back_tiles(sz, 0, first, count, qs, kvs, dos, kept, grad_q, grad_kv, key_t)
 
 
@@ -456,7 +456,7 @@
         out[src, 0 : sz.slot, :] = jnp.where(real, jnp.where(left, swap_halves(both), kv), 0.0).astype(BF16)
         out[src, sz.slot :, :] = fold_head(both[: sz.rows], sz, False).astype(BF16)
 
-    loop(sz.n, pack)
+    loop(sz.n, pack, 4)
 
 
 def attend_back_first(sz, first, count, recv_grad, qs, kvs, kept):

time: 411 us -> 398 us (0.968)
  Pallas kernels: 193 us -> 164 us
  waiting for transfers between devices: 55.7 us -> 69.8 us
    ppermute x12, waiting for transfers between devices: 10.3 us -> 25 us  [send(): lax.ppermute(block, 'seq', [(i, i ^ bit) for i in range(sz.n)])]
    pallas_call x1, Pallas kernels: 47.8 us -> 33.7 us  [attend_back_first(): pl.pallas_call(lambda *refs: back_first_kernel(sz, *refs), in_specs=[smem...]
    pallas_call x1, Pallas kernels: 35 us -> 25.6 us  [attend(): pl.pallas_call(lambda *refs: attend_kernel(sz, *refs), in_specs=[smem, sm...]
    pallas_call x1, Pallas kernels: 24.6 us -> 19.6 us  [attend_back_last(): pl.pallas_call(lambda *refs: back_last_kernel(sz, *refs), in_specs=[smem,...]
  transfers between devices with their start and end apart: 31 -> 31, of which waited for: 7 -> 10; matrix products, arithmetic and copies ran while one was open for 4% -> 4% of each run, Pallas kernels for 44% -> 38%
where the time goes in v2:
time: 398 us; the launch traced here: 394 us
  Pallas kernels  164 us (41%)
  waiting for transfers between devices  69.8 us (18%)
  blocking collectives  63.6 us (16%)
  starting transfers between devices  39.1 us (10%)
  local copies, waits for them, and re-layouts  32.7 us (8%)
  between operations  15.2 us (4%)
  other arithmetic  5.31 us (1%)
  matrix products  4.39 us (1%)
    all_to_all x1, blocking collectives, exchange(): return lax.all_to_all(message, 'seq', 0, 0, tiled=True)  63.6 us
    pallas_call x1, Pallas kernels, attend_back_first(): pl.pallas_call(lambda *refs: back_first_kernel(sz, *refs), in_specs=[smem...  33.7 us
    pallas_call x1, Pallas kernels, feed(): pl.pallas_call(lambda *refs: feed_kernel(sz, *refs), grid=(steps,), in_sp...  26.9 us
    pallas_call x1, Pallas kernels, attend(): pl.pallas_call(lambda *refs: attend_kernel(sz, *refs), in_specs=[smem, sm...  25.6 us
    ppermute x12, waiting for transfers between devices, send(): lax.ppermute(block, 'seq', [(i, i ^ bit) for i in range(sz.n)])  25 us
    unnamed x98, local copies, waits for them, and re-layouts  24.1 us
    all_to_all x1, waiting for transfers between devices, per_device(): heads_in = lax.all_to_all(out_message, 'seq', 0, 0, tiled=True)[::sz.rep]  23.1 us
    pallas_call x1, Pallas kernels, attend_back_last(): pl.pallas_call(lambda *refs: back_last_kernel(sz, *refs), in_specs=[smem,...  19.6 us
  transfers between devices with their start and end apart: 31, of which 10 were waited for; matrix products, arithmetic and copies ran while one was open for 4% of the time, Pallas kernels for 38%

profile of v2, /device:TPU:0, one launch (start us, length us, event | category | flops | bytes accessed | tf_op | source)
XLA Modules:
  0.0 394.2 jit_solution(3759086865877590020)
XLA Ops:
  9.7 9.7 %project.1 = (bf16[16,608,128]{2,1,0:T(8,128)(2,1)}, bf16[400,1024]{1,0:T(8,128)(2,1)}) custom-call(s32[8]{0:T(128)} %pad_add_fusion.2.refs_0_, bf16[392,1024]{1,0:T(8,128)(2,1)} %bitcast.240, f32[1,1024]{1,0:T(1,128)} %bitcast.228, f32[1,1024]{1,0:T(1,128)} %bitcast.227, bf16[1024,3072]{1,0:T(8,128)(2,1)} %refs_4_.3, bf16[1024,3072]{1,0:T(8,128)(2,1)} %refs_4_.3, ...), custom_call_target="tpu_custom_call" | custom-call | flops 9200000000 | bytes 1048576 | tf_op jit(solution)/shard_map/project/pallas_call | solution.py:258
  19.4 63.6 %all_to_all.20.refs_2_ = bf16[16,608,128]{2,1,0:T(8,128)(2,1)S(1)} all-to-all(bf16[16,608,128]{2,1,0:T(8,128)(2,1)} %get-tuple-element.274), channel_id=1, replica_groups=mesh['seq'=16,'dp'=2] {'seq'}, dimensions={0} | all-to-all | bytes 4980736 | tf_op jit(solution)/shard_map/all_to_all | solution.py:1082
  85.9 25.6 %attend.1 = (bf16[16,208,128]{2,1,0:T(8,128)(2,1)}, f32[6656,128]{1,0:T(8,128)}, bf16[6656,128]{1,0:T(8,128)(2,1)}, bf16[6400,128]{1,0:T(8,128)(2,1)}) custom-call(s32[8]{0:T(128)} %bitcast.205, s32[8]{0:T(128)} %bitcast.208, bf16[16,608,128]{2,1,0:T(8,128)(2,1)} %copy-done.37), custom_call_target="tpu_custom_call" | custom-call | flops 36800000000 | bytes 1048576 | tf_op jit(solution)/shard_map/attend/pallas_call | solution.py:364
  111.5 4.6 %all-to-all-start.1 = ((bf16[16,208,128]{2,1,0:T(8,128)(2,1)}), bf16[16,208,128]{2,1,0:T(8,128)(2,1)S(1)}, u32[]{:S(2)}, u32[]{:S(2)}) async-start(bf16[16,208,128]{2,1,0:T(8,128)(2,1)} %get-tuple-element.275), calls=%async_computation.1 | async-start | bytes 1703936 | tf_op jit(solution)/shard_map/all_to_all | solution.py:1101
  117.4 2.3 constant_dynamic-slice_fusion.6
  121.0 1.1 reshape.600
  122.2 4.4 %fusion.2.refs_8_ = f32[6400,128]{1,0:T(8,128)} fusion(pred[6400,48]{0,1:T(8,128)(4,1)S(1)} %reshape.600, f32[16,128]{1,0:T(8,128)S(1)} %get-tuple-element.380, f32[16,128]{1,0:T(8,128)S(1)} %get-tuple-element.379, f32[16,128]{1,0:T(8,128)S(1)} %get-tuple-element.378), kind=kOutput, calls=%fused_computation.20 | convolution fusion | flops 471871488 | bytes 3608576 | tf_op jit(solution)/shard_map/dot_general | solution.py:108
  126.5 23.1 %all-to-all-done.1.refs_2_ = bf16[16,208,128]{2,1,0:T(8,128)(2,1)S(1)} async-done(((bf16[16,208,128]{2,1,0:T(8,128)(2,1)}), bf16[16,208,128]{2,1,0:T(8,128)(2,1)S(1)}, u32[]{:S(2)}, u32[]{:S(2)}) %all-to-all-start.1) | async-done | bytes 852000 | tf_op jit(solution)/shard_map/all_to_all | solution.py:1101
  150.7 26.9 %feed.1 = (bf16[392,1024]{1,0:T(8,128)(2,1)}, f32[392,1024]{1,0:T(8,128)}, bf16[16,208,128]{2,1,0:T(8,128)(2,1)}, bf16[392,3072]{1,0:T(8,128)(2,1)}, bf16[392,40...) custom-call(s32[6]{0:T(128)} %stack.64.refs_0_, ...), custom_call_target="tpu_custom_call" | custom-call | flops 32199999488 | bytes 1048576 | tf_op jit(solution)/shard_map/feed/pallas_call | solution.py:645
  178.6 3.8 all-to-all-start.2
  182.4 8.2 %collective-permute-done.1.refs_4_ = bf16[392,1024]{1,0:T(8,128)(2,1)} collective-permute-done((bf16[392,1024]{1,0:T(8,128)(2,1)}, bf16[392,1024]{1,0:T(8,128)(2,1)}, u32[]{:S(2)}, u32[]{:S(2)}) %collective-permute-start.1) | collective-permute-done | bytes 802848 | tf_op jit(solution)/shard_map/ppermute | solution.py:1077
  190.7 1.4 copy-done.45
  192.1 18.3 %weights.1 = (bf16[4,256,1024]{2,1,0:T(8,128)(2,1)}, bf16[4,256,1024]{2,1,0:T(8,128)(2,1)}, bf16[8,2,32,1024]{3,2,1,0:T(8,128)(2,1)}, bf16[8,2,32,1024]{3,2,1,0:...) custom-call(s32[6]{0:T(128)} %stack.64.refs_0_, ...), custom_call_target="tpu_custom_call" | custom-call | flops 11500000256 | bytes 1048576 | tf_op jit(solution)/shard_map/weights/pallas_call | solution.py:765
  210.4 2.9 collective-permute-start.7
  213.3 1.2 collective-permute-start.4
  214.5 2.0 copy-done.31
  216.5 1.5 copy-done.33
  218.0 1.4 copy-done.34
  219.4 33.7 %attend_back_first.1 = (bf16[6656,128]{1,0:T(8,128)(2,1)S(1)}, f32[6656,128]{1,0:T(8,128)S(1)}, f32[6400,128]{1,0:T(8,128)S(1)}) custom-call(s32[8]{0:T(128)S(1)} %bitcast.206, s32[8]{0:T(128)S(1)} %bitcast.209, bf16[16,208,128]{2,1,0:T(8,128)(2,1)S(1)} %all-to-all-done.2.refs_2_, bf16[6656,128]{1,0:T(8,128)(2,1)S(1)} %copy-done.33, ...), custom_call_target="tpu_custom_call" | custom-call | flops 46000001024 | bytes 1048576 | tf_op jit(solution)/shard_map/attend_back_first/pallas_call | solution.py:466
  253.2 6.0 %collective-permute-done.6 = bf16[8,2,32,1024]{3,2,1,0:T(8,128)(2,1)S(1)} collective-permute-done((bf16[8,2,32,1024]{3,2,1,0:T(8,128)(2,1)}, bf16[8,2,32,1024]{3,2,1,0:T(8,128)(2,1)S(1)}, u32[]{:S(2)}, u32[]{:S(2)}) %collective-permute-start.6) | collective-permute-done | bytes 1048608 | tf_op jit(solution)/shard_map/ppermute | solution.py:932
  259.2 2.6 collective-permute-done.5
  261.9 1.6 halve.3
  265.8 1.7 collective-permute-start.11
  268.3 1.7 collective-permute-start.8
  269.9 19.6 %attend_back_last.1.refs_0_ = bf16[16,608,128]{2,1,0:T(8,128)(2,1)} custom-call(s32[8]{0:T(128)S(1)} %bitcast.207, s32[8]{0:T(128)S(1)} %bitcast.210, bf16[6656,128]{1,0:T(8,128)(2,1)S(1)} %get-tuple-element.305.refs_2_, bf16[6656,128]{1,0:T(8,128)(2,1)S(1)} %copy-done.33, bf16[6400,128]{1,0:T(8,128)(2,1)S(1)} %copy-done.35, f32[6656,128]{1,0:T(8,128)S(1)} %copy-done.32, ...), custom_call_target="tpu_custom_call" | custom-call | flops 23000000512 | bytes 1048576 | tf_op jit(solution)/shard_map/attend_back_last/pallas_call | solution.py:486
  291.8 5.5 %collective-permute-done.8 = bf16[2,256,1024]{2,1,0:T(8,128)(2,1)S(1)} collective-permute-done((bf16[2,256,1024]{2,1,0:T(8,128)(2,1)S(1)}, bf16[2,256,1024]{2,1,0:T(8,128)(2,1)S(1)}, u32[]{:S(2)}, u32[]{:S(2)}) %collective-permute-start.8) | collective-permute-done | bytes 1048608 | tf_op jit(solution)/shard_map/ppermute | solution.py:932
  297.3 4.7 %all-to-all-start.3 = ((bf16[16,608,128]{2,1,0:T(8,128)(2,1)}), bf16[16,608,128]{2,1,0:T(8,128)(2,1)}, u32[]{:S(2)}, u32[]{:S(2)}) async-start(bf16[16,608,128]{2,1,0:T(8,128)(2,1)} %attend_back_last.1.refs_0_), calls=%async_computation.3 | async-start | bytes 4980736 | tf_op jit(solution)/shard_map/all_to_all | solution.py:1171
  303.1 1.0 copy-done.10
  304.1 1.0 copy-done.12
  305.2 1.0 copy-done.14
  308.1 1.2 halve.4
  313.5 1.3 collective-permute-start.12
  314.8 1.9 collective-permute-start.13
  318.0 12.1 %triple_grad.1 = f32[1024,256]{1,0:T(8,128)} custom-call(bf16[16,608,128]{2,1,0:T(8,128)(2,1)} %attend_back_last.1.refs_0_, bf16[16,400,1024]{2,1,0:T(8,128)(2,1)} %bitcast.211), custom_call_target="tpu_custom_call" | custom-call | flops 1150000000 | bytes 1048576 | tf_op jit(solution)/shard_map/triple_grad/pallas_call | solution.py:543
  330.1 4.3 %collective-permute-done.15 = bf16[2,32,1024]{2,1,0:T(8,128)(2,1)S(1)} collective-permute-done((bf16[2,32,1024]{2,1,0:T(8,128)(2,1)}, bf16[2,32,1024]{2,1,0:T(8,128)(2,1)S(1)}, u32[]{:S(2)}, u32[]{:S(2)}) %collective-permute-start.15) | collective-permute-done | bytes 131104 | tf_op jit(solution)/shard_map/ppermute | solution.py:932
  335.1 1.9 multiply_reduce_fusion
  337.5 1.1 collective-permute-start.16
  338.6 7.3 %collective-permute-done.16 = bf16[16,32,256]{2,1,0:T(8,128)(2,1)S(1)} collective-permute-done((bf16[16,32,256]{2,1,0:T(8,128)(2,1)S(1)}, bf16[16,32,256]{2,1,0:T(8,128)(2,1)S(1)}, u32[]{:S(2)}, u32[]{:S(2)}) %collective-permute-start.16) | collective-permute-done | bytes 262176 | tf_op jit(solution)/shard_map/ppermute | solution.py:1190
  346.1 1.5 collective-permute-start.18
  348.2 4.9 %collective-permute-done.18 = bf16[4,32,256]{2,1,0:T(8,128)(2,1)S(1)} collective-permute-done((bf16[4,32,256]{2,1,0:T(8,128)(2,1)S(1)}, bf16[4,32,256]{2,1,0:T(8,128)(2,1)S(1)}, u32[]{:S(2)}, u32[]{:S(2)}) %collective-permute-start.18) | collective-permute-done | bytes 65568 | tf_op jit(solution)/shard_map/ppermute | solution.py:936
  353.1 1.1 collective-permute-done.19
  354.4 3.5 collective-permute-start.21
  358.8 3.3 halve.5
  362.1 3.5 collective-permute-start.25
  365.7 1.4 collective-permute-start.23
  367.2 8.9 %finish.1 = f32[392,1024]{1,0:T(8,128)} custom-call(bf16[16,608,128]{2,1,0:T(8,128)(2,1)} %all-to-all-done.3.refs_0_, bf16[1024,3072]{1,0:T(8,128)(2,1)} %refs_4_.3, bf16[1024,3072]{1,0:T(8,128)(2,1)} %refs_4_.3, bf16[1024,3072]{1,0:T(8,128)(2,1)} %refs_4_.3, bf16[392,1024]{1,0:T(8,128)(2,1)} %bitcast.242, f32[1,1024]{1,0:T(1,128)} %bitcast.229, ...), custom_call_target="tpu_custom_call" | custom-call | flops 11500000256 | bytes 1048576 | tf_op jit(solution)/shard_map/finish/pallas_call | solution.py:825
  376.0 6.5 %collective-permute-done.23 = bf16[1,128,1024]{2,1,0:T(8,128)(2,1)S(1)} collective-permute-done((bf16[1,128,1024]{2,1,0:T(8,128)(2,1)}, bf16[1,128,1024]{2,1,0:T(8,128)(2,1)S(1)}, u32[]{:S(2)}, u32[]{:S(2)}) %collective-permute-start.23) | collective-permute-done | bytes 262176 | tf_op jit(solution)/shard_map/ppermute | solution.py:932
  382.6 3.4 last.1
  (200 shorter events, 27.6 us)
Async XLA Ops:
  7.2 310.7 %all-gather.3.cloned.1.call-start = ((), (), s32[]{:S(2)}) async-start(), calls=%async_computation.4 | async-start | bytes 13926400 | tf_op jit(solution)/shard_map/all_gather | solution.py:1096
  111.5 38.2 %all-to-all-start.1 = ((bf16[16,208,128]{2,1,0:T(8,128)(2,1)}), bf16[16,208,128]{2,1,0:T(8,128)(2,1)S(1)}, u32[]{:S(2)}, u32[]{:S(2)}) async-start(bf16[16,208,128]{2,1,0:T(8,128)(2,1)} %get-tuple-element.275), calls=%async_computation.1 | async-start | bytes 1703936 | tf_op jit(solution)/shard_map/all_to_all | solution.py:1101
  177.5 13.1 %collective-permute-start.2 = (bf16[392,4096]{1,0:T(8,128)(2,1)}, bf16[392,4096]{1,0:T(8,128)(2,1)}, u32[]{:S(2)}, u32[]{:S(2)}) collective-permute-start(bf16[392,4096]{1,0:T(8,128)(2,1)} %get-tuple-element.281.refs_5_), channel_id=1, source_target_pairs={{0,2},{2,0},{4,6},{6,4},{8,10},{10,8},{12,14},{14,12},{16,18},{18,... | collective-permute-start | bytes 9633800 | tf_op jit(solution)/shard_map/ppermute | solution.py:1077
  177.6 13.1 %collective-permute-start.3 = (bf16[392,3072]{1,0:T(8,128)(2,1)}, bf16[392,3072]{1,0:T(8,128)(2,1)S(1)}, u32[]{:S(2)}, u32[]{:S(2)}) collective-permute-start(bf16[392,3072]{1,0:T(8,128)(2,1)} %get-tuple-element.282.refs_7_.refs_9_.refs_11_), channel_id=1, source_target_pairs={{0,2},{2,0},{4,6},{6,4},{8,10},{10,8},{12,14},{14,12},{16,18},{18,... | collective-permute-start | bytes 7225352 | tf_op jit(solution)/shard_map/ppermute | solution.py:1077
  178.1 12.6 %collective-permute-start = (bf16[392,2048]{1,0:T(8,128)(2,1)}, bf16[392,2048]{1,0:T(8,128)(2,1)}, u32[]{:S(2)}, u32[]{:S(2)}) collective-permute-start(bf16[392,2048]{1,0:T(8,128)(2,1)} %get-tuple-element.280), channel_id=1, source_target_pairs={{0,2},{2,0},{4,6},{6,4},{8,10},{10,8},{12,14},{14,12},{16,18},{18,... | collective-permute-start | bytes 4816904 | tf_op jit(solution)/shard_map/ppermute | solution.py:1077
  178.2 12.5 %collective-permute-start.1 = (bf16[392,1024]{1,0:T(8,128)(2,1)}, bf16[392,1024]{1,0:T(8,128)(2,1)}, u32[]{:S(2)}, u32[]{:S(2)}) collective-permute-start(bf16[392,1024]{1,0:T(8,128)(2,1)} %bitcast.238), channel_id=1, source_target_pairs={{0,2},{2,0},{4,6},{6,4},{8,10},{10,8},{12,14},{14,12},{16,18},{18,... | collective-permute-start | bytes 2408456 | tf_op jit(solution)/shard_map/ppermute | solution.py:1077
  178.6 31.7 %all-to-all-start.2 = ((bf16[16,208,128]{2,1,0:T(8,128)(2,1)}), bf16[16,208,128]{2,1,0:T(8,128)(2,1)S(1)}, u32[]{:S(2)}, u32[]{:S(2)}) async-start(bf16[16,208,128]{2,1,0:T(8,128)(2,1)} %get-tuple-element.278), calls=%async_computation.2 | async-start | bytes 1703936 | tf_op jit(solution)/shard_map/all_to_all | solution.py:1082
  192.1 22.5 %copy-start.29 = (s32[8,1]{0,1:T(1,128)S(1)}, s32[8,1]{0,1:T(1,128)}, u32[]{:S(2)}) copy-start(s32[8,1]{0,1:T(1,128)} %slice.200) | copy-start | bytes 100
  192.1 22.5 %copy-start.30 = (s32[8,1]{0,1:T(1,128)S(1)}, s32[8,1]{0,1:T(1,128)}, u32[]{:S(2)}) copy-start(s32[8,1]{0,1:T(1,128)} %slice.201) | copy-start | bytes 100
  210.4 42.8 %collective-permute-start.7 = (bf16[8,32,1024]{2,1,0:T(8,128)(2,1)}, bf16[8,32,1024]{2,1,0:T(8,128)(2,1)S(1)}, u32[]{:S(2)}, u32[]{:S(2)}) collective-permute-start(bf16[8,32,1024]{2,1,0:T(8,128)(2,1)} %get-tuple-element.299), channel_id=1, source_target_pairs={{0,1},{1,0},{2,3},{3,2},{4,5},{5,4},{6,7},{7,6},{8,9},{9,8},{10,11... | collective-permute-start | bytes 1572872 | tf_op jit(solution)/shard_map/ppermute | solution.py:928
  213.3 45.9 %collective-permute-start.6 = (bf16[8,2,32,1024]{3,2,1,0:T(8,128)(2,1)}, bf16[8,2,32,1024]{3,2,1,0:T(8,128)(2,1)S(1)}, u32[]{:S(2)}, u32[]{:S(2)}) collective-permute-start(bf16[8,2,32,1024]{3,2,1,0:T(8,128)(2,1)} %get-tuple-element.297), channel_id=1, source_target_pairs={{0,8},{2,10},{4,12},{6,14},{8,0},{10,2},{12,4},{14,6},{16,24},{18,... | collective-permute-start | bytes 3145736 | tf_op jit(solution)/shard_map/ppermute | solution.py:932
  213.3 48.5 %collective-permute-start.5 = (bf16[8,2,32,1024]{3,2,1,0:T(8,128)(2,1)}, bf16[8,2,32,1024]{3,2,1,0:T(8,128)(2,1)S(1)}, u32[]{:S(2)}, u32[]{:S(2)}) collective-permute-start(bf16[8,2,32,1024]{3,2,1,0:T(8,128)(2,1)} %get-tuple-element.294), channel_id=1, source_target_pairs={{0,16},{2,18},{4,20},{6,22},{8,24},{10,26},{12,28},{14,30},{16,0},... | collective-permute-start | bytes 3145736 | tf_op jit(solution)/shard_map/ppermute | solution.py:932
  213.3 48.5 %collective-permute-start.4 = (bf16[4,256,1024]{2,1,0:T(8,128)(2,1)}, bf16[4,256,1024]{2,1,0:T(8,128)(2,1)S(1)}, u32[]{:S(2)}, u32[]{:S(2)}) collective-permute-start(bf16[4,256,1024]{2,1,0:T(8,128)(2,1)} %get-tuple-element.290), channel_id=1, source_target_pairs={{0,4},{2,6},{4,0},{6,2},{8,12},{10,14},{12,8},{14,10},{16,20},{18,... | collective-permute-start | bytes 6291464 | tf_op jit(solution)/shard_map/ppermute | solution.py:932
  219.4 42.5 %copy-start = (bf16[4,256,1024]{2,1,0:T(8,128)(2,1)S(1)}, bf16[4,256,1024]{2,1,0:T(8,128)(2,1)}, u32[]{:S(2)}) copy-start(bf16[4,256,1024]{2,1,0:T(8,128)(2,1)} %get-tuple-element.289) | copy-start | bytes 6291460
  219.4 42.5 %copy-start.1 = (bf16[8,2,32,1024]{3,2,1,0:T(8,128)(2,1)S(1)}, bf16[8,2,32,1024]{3,2,1,0:T(8,128)(2,1)}, u32[]{:S(2)}) copy-start(bf16[8,2,32,1024]{3,2,1,0:T(8,128)(2,1)} %get-tuple-element.293) | copy-start | bytes 3145732
  219.4 42.5 %copy-start.2 = (bf16[8,2,32,1024]{3,2,1,0:T(8,128)(2,1)S(1)}, bf16[8,2,32,1024]{3,2,1,0:T(8,128)(2,1)}, u32[]{:S(2)}) copy-start(bf16[8,2,32,1024]{3,2,1,0:T(8,128)(2,1)} %get-tuple-element.296) | copy-start | bytes 3145732
  219.4 42.5 %copy-start.4 = (bf16[8,32,1024]{2,1,0:T(8,128)(2,1)S(1)}, bf16[8,32,1024]{2,1,0:T(8,128)(2,1)}, u32[]{:S(2)}) copy-start(bf16[8,32,1024]{2,1,0:T(8,128)(2,1)} %get-tuple-element.283) | copy-start | bytes 1572868
  219.4 42.5 %copy-start.5 = (s32[6]{0:T(128)S(1)}, s32[6]{0:T(128)}, u32[]{:S(2)}) copy-start(s32[6]{0:T(128)} %stack.64.refs_0_) | copy-start | bytes 76
  265.8 23.7 %collective-permute-start.11 = (bf16[1,128,1024]{2,1,0:T(8,128)(2,1)S(1)}, bf16[1,128,1024]{2,1,0:T(8,128)(2,1)S(1)}, u32[]{:S(2)}, u32[]{:S(2)}) collective-permute-start(bf16[1,128,1024]{2,1,0:T(8,128)(2,1)S(1)} %get-tuple-element.304), channel_id=1, source_target_pairs={{0,16},{2,18},{4,20},{6,22},{8,24},{10,26},{12,28},{14,30},{16,0},... | collective-permute-start | bytes 786440 | tf_op jit(solution)/shard_map/ppermute | solution.py:932
  267.5 22.7 %collective-permute-start.10 = (bf16[2,128,1024]{2,1,0:T(8,128)(2,1)S(1)}, bf16[2,128,1024]{2,1,0:T(8,128)(2,1)S(1)}, u32[]{:S(2)}, u32[]{:S(2)}) collective-permute-start(bf16[2,128,1024]{2,1,0:T(8,128)(2,1)S(1)} %get-tuple-element.303), channel_id=1, source_target_pairs={{0,4},{2,6},{4,0},{6,2},{8,12},{10,14},{12,8},{14,10},{16,20},{18,... | collective-permute-start | bytes 1572872 | tf_op jit(solution)/shard_map/ppermute | solution.py:932
  267.8 23.2 %collective-permute-start.9 = (bf16[4,64,1024]{2,1,0:T(8,128)(2,1)S(1)}, bf16[4,64,1024]{2,1,0:T(8,128)(2,1)S(1)}, u32[]{:S(2)}, u32[]{:S(2)}) collective-permute-start(bf16[4,64,1024]{2,1,0:T(8,128)(2,1)S(1)} %get-tuple-element.302), channel_id=1, source_target_pairs={{0,1},{1,0},{2,3},{3,2},{4,5},{5,4},{6,7},{7,6},{8,9},{9,8},{10,11... | collective-permute-start | bytes 1572872 | tf_op jit(solution)/shard_map/ppermute | solution.py:928
  268.3 29.1 %collective-permute-start.8 = (bf16[2,256,1024]{2,1,0:T(8,128)(2,1)S(1)}, bf16[2,256,1024]{2,1,0:T(8,128)(2,1)S(1)}, u32[]{:S(2)}, u32[]{:S(2)}) collective-permute-start(bf16[2,256,1024]{2,1,0:T(8,128)(2,1)S(1)} %get-tuple-element.301), channel_id=1, source_target_pairs={{0,8},{2,10},{4,12},{6,14},{8,0},{10,2},{12,4},{14,6},{16,24},{18,... | collective-permute-start | bytes 3145736 | tf_op jit(solution)/shard_map/ppermute | solution.py:932
  297.3 64.7 %all-to-all-start.3 = ((bf16[16,608,128]{2,1,0:T(8,128)(2,1)}), bf16[16,608,128]{2,1,0:T(8,128)(2,1)}, u32[]{:S(2)}, u32[]{:S(2)}) async-start(bf16[16,608,128]{2,1,0:T(8,128)(2,1)} %attend_back_last.1.refs_0_), calls=%async_computation.3 | async-start | bytes 4980736 | tf_op jit(solution)/shard_map/all_to_all | solution.py:1171
  313.5 21.0 %collective-permute-start.12 = (bf16[2,128,1024]{2,1,0:T(8,128)(2,1)S(1)}, bf16[2,128,1024]{2,1,0:T(8,128)(2,1)S(1)}, u32[]{:S(2)}, u32[]{:S(2)}) collective-permute-start(bf16[2,128,1024]{2,1,0:T(8,128)(2,1)S(1)} %get-tuple-element.316), channel_id=1, source_target_pairs={{0,1},{1,0},{2,3},{3,2},{4,5},{5,4},{6,7},{7,6},{8,9},{9,8},{10,11... | collective-permute-start | bytes 1572872 | tf_op jit(solution)/shard_map/ppermute | solution.py:928
  314.8 19.7 %collective-permute-start.13 = (bf16[2,64,1024]{2,1,0:T(8,128)(2,1)}, bf16[2,64,1024]{2,1,0:T(8,128)(2,1)}, u32[]{:S(2)}, u32[]{:S(2)}) collective-permute-start(bf16[2,64,1024]{2,1,0:T(8,128)(2,1)} %copy-done.15), channel_id=1, source_target_pairs={{0,4},{2,6},{4,0},{6,2},{8,12},{10,14},{12,8},{14,10},{16,20},{18,... | collective-permute-start | bytes 786440 | tf_op jit(solution)/shard_map/ppermute | solution.py:932
  316.6 17.8 %collective-permute-start.14 = (bf16[2,64,1024]{2,1,0:T(8,128)(2,1)S(1)}, bf16[2,64,1024]{2,1,0:T(8,128)(2,1)}, u32[]{:S(2)}, u32[]{:S(2)}) collective-permute-start(bf16[2,64,1024]{2,1,0:T(8,128)(2,1)S(1)} %get-tuple-element.318), channel_id=1, source_target_pairs={{0,1},{1,0},{2,3},{3,2},{4,5},{5,4},{6,7},{7,6},{8,9},{9,8},{10,11... | collective-permute-start | bytes 786440 | tf_op jit(solution)/shard_map/ppermute | solution.py:928
  317.4 17.0 %collective-permute-start.15 = (bf16[2,32,1024]{2,1,0:T(8,128)(2,1)}, bf16[2,32,1024]{2,1,0:T(8,128)(2,1)S(1)}, u32[]{:S(2)}, u32[]{:S(2)}) collective-permute-start(bf16[2,32,1024]{2,1,0:T(8,128)(2,1)} %copy-done.20), channel_id=1, source_target_pairs={{0,4},{2,6},{4,0},{6,2},{8,12},{10,14},{12,8},{14,10},{16,20},{18,... | collective-permute-start | bytes 393224 | tf_op jit(solution)/shard_map/ppermute | solution.py:932
  317.9 17.2 %copy-start.38 = (bf16[1024,64]{1,0:T(8,128)(2,1)S(1)}, bf16[1024,64]{1,0:T(8,128)(2,1)}, u32[]{:S(2)}) copy-start(bf16[1024,64]{1,0:T(8,128)(2,1)} %get-tuple-element.365) | copy-start | bytes 393220
  317.9 17.2 %copy-start.39 = (bf16[1024,64]{1,0:T(8,128)(2,1)S(1)}, bf16[1024,64]{1,0:T(8,128)(2,1)}, u32[]{:S(2)}) copy-start(bf16[1024,64]{1,0:T(8,128)(2,1)} %get-tuple-element.366) | copy-start | bytes 393220
  318.0 17.2 %copy-start.40 = (bf16[1024,64]{1,0:T(8,128)(2,1)S(1)}, bf16[1024,64]{1,0:T(8,128)(2,1)}, u32[]{:S(2)}) copy-start(bf16[1024,64]{1,0:T(8,128)(2,1)} %get-tuple-element.367) | copy-start | bytes 393220
  337.1 10.9 %copy-start.44 = (f32[1024]{0:T(1024)S(1)}, f32[1024]{0:T(1024)}, u32[]{:S(2)}) copy-start(f32[1024]{0:T(1024)} %param.58) | copy-start | bytes 12292
  337.1 11.0 %copy-start.43 = (f32[1024]{0:T(1024)S(1)}, f32[1024]{0:T(1024)}, u32[]{:S(2)}) copy-start(f32[1024]{0:T(1024)} %param.59) | copy-start | bytes 12292
  337.5 8.4 %collective-permute-start.16 = (bf16[16,32,256]{2,1,0:T(8,128)(2,1)S(1)}, bf16[16,32,256]{2,1,0:T(8,128)(2,1)S(1)}, u32[]{:S(2)}, u32[]{:S(2)}) collective-permute-start(bf16[16,32,256]{2,1,0:T(8,128)(2,1)S(1)} %fusion.1), channel_id=1, source_target_pairs={{0,1},{1,0},{2,3},{3,2},{4,5},{5,4},{6,7},{7,6},{8,9},{9,8},{10,11... | collective-permute-start | bytes 786440 | tf_op jit(solution)/shard_map/ppermute | solution.py:1190
  346.0 2.2 collective-permute-start.17
  346.1 7.0 %collective-permute-start.18 = (bf16[4,32,256]{2,1,0:T(8,128)(2,1)S(1)}, bf16[4,32,256]{2,1,0:T(8,128)(2,1)S(1)}, u32[]{:S(2)}, u32[]{:S(2)}) collective-permute-start(bf16[4,32,256]{2,1,0:T(8,128)(2,1)S(1)} %get-tuple-element.374), channel_id=1, source_target_pairs={{0,4},{2,6},{4,0},{6,2},{8,12},{10,14},{12,8},{14,10},{16,20},{18,... | collective-permute-start | bytes 196616 | tf_op jit(solution)/shard_map/ppermute | solution.py:936
  347.6 6.6 %collective-permute-start.19 = (bf16[4,32,256]{2,1,0:T(8,128)(2,1)S(1)}, bf16[4,32,256]{2,1,0:T(8,128)(2,1)S(1)}, u32[]{:S(2)}, u32[]{:S(2)}) collective-permute-start(bf16[4,32,256]{2,1,0:T(8,128)(2,1)S(1)} %get-tuple-element.373), channel_id=1, source_target_pairs={{0,6},{2,4},{4,2},{6,0},{8,14},{10,12},{12,10},{14,8},{16,22},{18,... | collective-permute-start | bytes 196616 | tf_op jit(solution)/shard_map/ppermute | solution.py:936
  354.3 11.3 %collective-permute-start.20 = (bf16[4,32,256]{2,1,0:T(8,128)(2,1)S(1)}, bf16[4,32,256]{2,1,0:T(8,128)(2,1)S(1)}, u32[]{:S(2)}, u32[]{:S(2)}) collective-permute-start(bf16[4,32,256]{2,1,0:T(8,128)(2,1)S(1)} %get-tuple-element.371), channel_id=1, source_target_pairs={{0,8},{2,10},{4,12},{6,14},{8,0},{10,2},{12,4},{14,6},{16,24},{18,... | collective-permute-start | bytes 196616 | tf_op jit(solution)/shard_map/ppermute | solution.py:936
  354.4 11.3 %collective-permute-start.21 = (bf16[4,32,256]{2,1,0:T(8,128)(2,1)S(1)}, bf16[4,32,256]{2,1,0:T(8,128)(2,1)S(1)}, u32[]{:S(2)}, u32[]{:S(2)}) collective-permute-start(bf16[4,32,256]{2,1,0:T(8,128)(2,1)S(1)} %get-tuple-element.370), channel_id=1, source_target_pairs={{0,16},{2,18},{4,20},{6,22},{8,24},{10,26},{12,28},{14,30},{16,0},... | collective-permute-start | bytes 196616 | tf_op jit(solution)/shard_map/ppermute | solution.py:936
  357.9 9.2 %collective-permute-start.22 = (bf16[4,32,256]{2,1,0:T(8,128)(2,1)S(1)}, bf16[4,32,256]{2,1,0:T(8,128)(2,1)S(1)}, u32[]{:S(2)}, u32[]{:S(2)}) collective-permute-start(bf16[4,32,256]{2,1,0:T(8,128)(2,1)S(1)} %get-tuple-element.369), channel_id=1, source_target_pairs={{0,24},{2,26},{4,28},{6,30},{8,16},{10,18},{12,20},{14,22},{16,8},... | collective-permute-start | bytes 196616 | tf_op jit(solution)/shard_map/ppermute | solution.py:936
  362.0 14.0 %collective-permute-start.26 = (bf16[1,32,1024]{2,1,0:T(8,128)(2,1)}, bf16[1,32,1024]{2,1,0:T(8,128)(2,1)S(1)}, u32[]{:S(2)}, u32[]{:S(2)}) collective-permute-start(bf16[1,32,1024]{2,1,0:T(8,128)(2,1)} %get-tuple-element.342), channel_id=1, source_target_pairs={{0,8},{2,10},{4,12},{6,14},{8,0},{10,2},{12,4},{14,6},{16,24},{18,... | collective-permute-start | bytes 196616 | tf_op jit(solution)/shard_map/ppermute | solution.py:932
  362.1 13.9 %collective-permute-start.25 = (bf16[1,64,1024]{2,1,0:T(8,128)(2,1)}, bf16[1,64,1024]{2,1,0:T(8,128)(2,1)S(1)}, u32[]{:S(2)}, u32[]{:S(2)}) collective-permute-start(bf16[1,64,1024]{2,1,0:T(8,128)(2,1)} %get-tuple-element.341), channel_id=1, source_target_pairs={{0,16},{2,18},{4,20},{6,22},{8,24},{10,26},{12,28},{14,30},{16,0},... | collective-permute-start | bytes 393224 | tf_op jit(solution)/shard_map/ppermute | solution.py:932
  365.6 10.4 %collective-permute-start.24 = (bf16[1,64,1024]{2,1,0:T(8,128)(2,1)}, bf16[1,64,1024]{2,1,0:T(8,128)(2,1)S(1)}, u32[]{:S(2)}, u32[]{:S(2)}) collective-permute-start(bf16[1,64,1024]{2,1,0:T(8,128)(2,1)} %get-tuple-element.340), channel_id=1, source_target_pairs={{0,8},{2,10},{4,12},{6,14},{8,0},{10,2},{12,4},{14,6},{16,24},{18,... | collective-permute-start | bytes 393224 | tf_op jit(solution)/shard_map/ppermute | solution.py:932
  365.7 16.8 %collective-permute-start.23 = (bf16[1,128,1024]{2,1,0:T(8,128)(2,1)}, bf16[1,128,1024]{2,1,0:T(8,128)(2,1)S(1)}, u32[]{:S(2)}, u32[]{:S(2)}) collective-permute-start(bf16[1,128,1024]{2,1,0:T(8,128)(2,1)} %get-tuple-element.339), channel_id=1, source_target_pairs={{0,16},{2,18},{4,20},{6,22},{8,24},{10,26},{12,28},{14,30},{16,0},... | collective-permute-start | bytes 786440 | tf_op jit(solution)/shard_map/ppermute | solution.py:932
  367.1 15.4 %copy-start.6 = (s32[6]{0:T(128)S(1)}, s32[6]{0:T(128)}, u32[]{:S(2)}) copy-start(s32[6]{0:T(128)} %stack.64.refs_0_) | copy-start | bytes 76
  367.1 15.4 %copy-start.24 = (bf16[1,128,1024]{2,1,0:T(8,128)(2,1)S(1)}, bf16[1,128,1024]{2,1,0:T(8,128)(2,1)}, u32[]{:S(2)}) copy-start(bf16[1,128,1024]{2,1,0:T(8,128)(2,1)} %get-tuple-element.345) | copy-start | bytes 786436
  367.1 15.4 %copy-start.26 = (bf16[1,64,1024]{2,1,0:T(8,128)(2,1)S(1)}, bf16[1,64,1024]{2,1,0:T(8,128)(2,1)}, u32[]{:S(2)}) copy-start(bf16[1,64,1024]{2,1,0:T(8,128)(2,1)} %get-tuple-element.347) | copy-start | bytes 393220
  367.1 15.4 %copy-start.27 = (bf16[1,64,1024]{2,1,0:T(8,128)(2,1)S(1)}, bf16[1,64,1024]{2,1,0:T(8,128)(2,1)}, u32[]{:S(2)}) copy-start(bf16[1,64,1024]{2,1,0:T(8,128)(2,1)} %get-tuple-element.349) | copy-start | bytes 393220
  367.1 15.4 %copy-start.28 = (bf16[1,32,1024]{2,1,0:T(8,128)(2,1)S(1)}, bf16[1,32,1024]{2,1,0:T(8,128)(2,1)}, u32[]{:S(2)}) copy-start(bf16[1,32,1024]{2,1,0:T(8,128)(2,1)} %get-tuple-element.351) | copy-start | bytes 196612
  (31 other events, 75.8 us)
Sparse Core Ops, SparseCore 0:
  83.2 86.0 all-gather.2
